TPU v7x, 128 devices: a whole 4x4x4 slice. The times are simulated.
128 devices in a mesh: dp: 32 (over y, x, z_lo), tensor: 4 (over z_hi, core).
Axes of the slice: x: 4, y: 4, z: 4 (z_hi: 2, z_lo: 2; z = z_hi * 2 + z_lo), core: 2. Of those that a mesh axis runs over, the one named last changes fastest.
Arguments:
- hidden_in: bfloat16 [32768, 1536], P(('dp', 'tensor')), may hold values from -6 to 6
- norm_gain: float32 [1536], replicated, may hold values from 0.1 to 1.9
- proj_zx: bfloat16 [1536, 2, 3072], P('dp', None, 'tensor'), may hold values from -0.15625 to 0.15625
- proj_shared: bfloat16 [1536, 256], P(('dp', 'tensor')), may hold values from -0.15625 to 0.15625
- proj_step: bfloat16 [1536, 48], P('dp', 'tensor'), may hold values from -0.15625 to 0.15625
- conv_inner: float32 [5, 3072], P(None, 'tensor'), may hold values from -0.5 to 0.5
- conv_shared: float32 [5, 256], replicated, may hold values from -0.5 to 0.5
- step_bias: float32 [48], P('tensor'), may hold values from -6 to -2
- decay_log: float32 [48], P('tensor'), may hold values from 0 to 2.7
- skip_gain: float32 [48], P('tensor'), may hold values from 0.5 to 1.5
- gated_gain: float32 [3072], P('tensor'), may hold values from 0.1 to 1.9
- proj_out: bfloat16 [3072, 1536], P('tensor', 'dp'), may hold values from -0.109375 to 0.109375
- out_grad: bfloat16 [32768, 1536], P(('dp', 'tensor')), may hold values from -6 to 6
- segments: int32 [32768], P('dp'), may hold values from 0 to 6, as said below
Outputs:
- hidden_out: bfloat16 [32768, 1536], P(('dp', 'tensor'))
- grad_hidden: bfloat16 [32768, 1536], P(('dp', 'tensor'))
- grad_norm_gain: float32 [1536], replicated
- grad_proj_zx: float32 [1536, 2, 3072], P('dp', None, 'tensor')
- grad_proj_shared: float32 [1536, 256], P(('dp', 'tensor'))
- grad_proj_step: float32 [1536, 48], P('dp', 'tensor')
- grad_conv_inner: float32 [5, 3072], P(None, 'tensor')
- grad_conv_shared: float32 [5, 256], replicated
- grad_step_bias: float32 [48], P('tensor')
- grad_decay_log: float32 [48], P('tensor')
- grad_skip_gain: float32 [48], P('tensor')
- grad_gated_gain: float32 [3072], P('tensor')
- grad_proj_out: float32 [3072, 1536], P('tensor', 'dp')
Inputs may be any that keep to these rules, and one draw needn't show every extreme that they name: `segments`: within each sequence of 1024 tokens the ids start at 0 and never fall; a document is a run of equal ids.
All inputs are finite; a program needn't handle non-finite values.
Results may differ from a plain program's by a relative error of at most 0.024.
Values may be sent and summed in bfloat16 or wider, within the bound.
No kernel may reach another device: no remote copies, remote signals or barrier semaphores. Data moves between devices by JAX's collectives and lax.ppermute only.
A program may use at most 256 MiB of HBM per device.

v0:
```python
from functools import partial

import jax
import jax.numpy as jnp
from jax import lax
from jax.sharding import PartitionSpec as P

SPAN = 256


EPS = 1e-05
HIGH = lax.Precision.HIGHEST


def causal_conv(values, conv_taps, segment_ids):
    length = values.shape[0]
    padded = jnp.concatenate([jnp.zeros((3, values.shape[1]), values.dtype), values], 0)
    seg_pad = jnp.concatenate([jnp.full((3,), -1, jnp.int32), segment_ids], 0)
    summed = conv_taps[4] + jnp.zeros_like(values)
    for offset in range(4):
        same_doc = (seg_pad[offset : offset + length] == segment_ids)[:, None]
        summed = summed + conv_taps[offset] * jnp.where(
            same_doc, padded[offset : offset + length], 0.0
        )
    return jax.nn.silu(summed)


def block_mixer(
    gate_pre,
    inner_pre,
    shared_pre,
    step_pre,
    conv_inner,
    conv_shared,
    step_bias,
    decay_log,
    skip_gain,
    segment_ids=None,
    block_len=None,
):
    inner_conv = causal_conv(inner_pre, conv_inner, segment_ids)
    shared_conv = causal_conv(shared_pre, conv_shared, segment_ids)
    length, inner_width = inner_conv.shape
    head_count = step_bias.shape[0]
    head_size = inner_width // head_count
    states = shared_conv.shape[1] // 2
    blocks = length // block_len
    step_sizes = jax.nn.softplus(step_pre + step_bias)
    log_decay = -step_sizes * jnp.exp(decay_log)
    inner_blocks = inner_conv.reshape(blocks, block_len, head_count, head_size)
    write_blocks = shared_conv[:, :states].reshape(blocks, block_len, states)
    read_blocks = shared_conv[:, states:].reshape(blocks, block_len, states)
    step_blocks = step_sizes.reshape(blocks, block_len, head_count)
    log_blocks = log_decay.reshape(blocks, block_len, head_count)
    doc_blocks = segment_ids.reshape(blocks, block_len)
    doc_before = jnp.concatenate([jnp.full((1,), -1, jnp.int32), doc_blocks[:-1, -1]], 0)
    places = jnp.arange(block_len)
    lower_tri = places[:, None] >= places[None, :]

    def advance(carried, operands):
        inner_here, write_here, read_here, step_here, log_here, doc_here, prior_doc = operands
        cumulative = jnp.cumsum(log_here, axis=0)
        allowed = lower_tri & (doc_here[:, None] == doc_here[None, :])
        inner_prod = jnp.dot(read_here, write_here.T, precision=HIGH)
        spread = jnp.where(
            allowed[None], cumulative.T[:, :, None] - cumulative.T[:, None, :], -jnp.inf
        )
        weights = jnp.exp(spread) * inner_prod[None] * step_here.T[:, None, :]
        within = jnp.einsum("hts,shp->thp", weights, inner_here, precision=HIGH)
        enters = jnp.where((doc_here == prior_doc)[:, None], jnp.exp(cumulative), 0.0)
        from_state = (
            jnp.einsum("tn,hnp->thp", read_here, carried, precision=HIGH) * enters[:, :, None]
        )
        result = within + from_state + inner_here * skip_gain[None, :, None]
        to_end = (
            jnp.where(
                (doc_here == doc_here[-1])[:, None],
                jnp.exp(cumulative[-1][None, :] - cumulative),
                0.0,
            )
            * step_here
        )
        carry_keep = jnp.where(doc_here[-1] == prior_doc, jnp.exp(cumulative[-1]), 0.0)
        updated = carried * carry_keep[:, None, None] + jnp.einsum(
            "sn,shp->hnp", write_here, inner_here * to_end[:, :, None], precision=HIGH
        )
        return (updated, result)

    initial = jnp.zeros((head_count, states, head_size), jnp.float32)
    unused, outputs = lax.scan(
        advance,
        initial,
        (inner_blocks, write_blocks, read_blocks, step_blocks, log_blocks, doc_blocks, doc_before),
    )
    return outputs.reshape(length, inner_width) * jax.nn.silu(gate_pre)


def per_device(
    hidden_in,
    norm_gain,
    proj_zx,
    proj_shared,
    proj_step,
    conv_inner,
    conv_shared,
    step_bias,
    decay_log,
    skip_gain,
    gated_gain,
    proj_out,
    out_grad,
    segments,
):
    residual_in = hidden_in.astype(jnp.float32)
    model_width = residual_in.shape[1]
    scale_in = lax.rsqrt(jnp.mean(residual_in * residual_in, axis=-1, keepdims=True) + EPS)
    normed_low = (residual_in * scale_in * norm_gain).astype(jnp.bfloat16)
    full_zx, full_step, full_out = (
        lax.all_gather(proj_zx, "dp", axis=0, tiled=True),
        lax.all_gather(proj_step, "dp", axis=0, tiled=True),
        lax.all_gather(proj_out, "dp", axis=1, tiled=True),
    )
    full_shared = lax.all_gather(proj_shared, ("dp", "tensor"), axis=0, tiled=True)
    token_rows = lax.all_gather(normed_low, "tensor", axis=0, tiled=True)
    grad_rows = lax.all_gather(out_grad, "tensor", axis=0, tiled=True)
    projected = jnp.einsum("td,dkc->tkc", token_rows, full_zx, preferred_element_type=jnp.float32)
    shared_pre = jnp.dot(token_rows, full_shared, preferred_element_type=jnp.float32)
    step_pre = jnp.dot(token_rows, full_step, preferred_element_type=jnp.float32)
    mixer_fn = partial(block_mixer, segment_ids=segments, block_len=SPAN)
    gated, mixer_back = jax.vjp(
        mixer_fn,
        projected[:, 0, :],
        projected[:, 1, :],
        shared_pre,
        step_pre,
        conv_inner,
        conv_shared,
        step_bias,
        decay_log,
        skip_gain,
    )
    inner_width = gated.shape[1] * lax.axis_size("tensor")
    square_sum = lax.psum(jnp.sum(gated * gated, axis=-1), "tensor")
    scale_mix = lax.rsqrt(square_sum / inner_width + EPS)[:, None]
    mixed_low = (gated * scale_mix * gated_gain).astype(jnp.bfloat16)
    mixed_sum = lax.psum_scatter(
        jnp.dot(mixed_low, full_out, preferred_element_type=jnp.float32).astype(jnp.bfloat16),
        "tensor",
        scatter_dimension=0,
        tiled=True,
    ).astype(jnp.float32)
    hidden_out = (residual_in + mixed_sum).astype(jnp.bfloat16)
    back_zx, back_step = (
        lax.all_gather(proj_zx, "dp", axis=0, tiled=True),
        lax.all_gather(proj_step, "dp", axis=0, tiled=True),
    )
    grad_out_full = lax.dot_general(
        mixed_low, grad_rows, (((0,), (0,)), ((), ())), preferred_element_type=jnp.float32
    )
    grad_mixed = lax.dot_general(
        grad_rows, full_out, (((1,), (1,)), ((), ())), preferred_element_type=jnp.float32
    )
    norm_dot = lax.psum(jnp.sum(grad_mixed * gated_gain * gated, axis=-1), "tensor")
    grad_gain_mix = jnp.sum(grad_mixed * gated * scale_mix, axis=0)
    grad_gated = (
        scale_mix * gated_gain * grad_mixed
        - gated * scale_mix**3 * (norm_dot / inner_width)[:, None]
    )
    (
        grad_gate,
        grad_inner,
        grad_shared,
        grad_step,
        grad_conv_in,
        grad_conv_sh,
        grad_bias,
        grad_decay,
        grad_skip,
    ) = mixer_back(grad_gated)
    grad_pair = jnp.stack([grad_gate, grad_inner], axis=1).astype(jnp.bfloat16)
    step_grad_low = grad_step.astype(jnp.bfloat16)
    grad_zx_full = jnp.einsum(
        "td,tkc->dkc", token_rows, grad_pair, preferred_element_type=jnp.float32
    )
    grad_step_full = lax.dot_general(
        token_rows, step_grad_low, (((0,), (0,)), ((), ())), preferred_element_type=jnp.float32
    )
    grad_token_rows = jnp.einsum(
        "tkc,dkc->td", grad_pair, back_zx, preferred_element_type=jnp.float32
    )
    grad_token_rows = grad_token_rows + lax.dot_general(
        step_grad_low, back_step, (((1,), (1,)), ((), ())), preferred_element_type=jnp.float32
    )
    mine_rows, mine_shared = (
        lax.psum_scatter(grad_token_rows, "tensor", scatter_dimension=0, tiled=True),
        lax.psum_scatter(grad_shared, "tensor", scatter_dimension=0, tiled=True),
    )
    shared_grad_low = mine_shared.astype(jnp.bfloat16)
    grad_normed = mine_rows + lax.dot_general(
        shared_grad_low, full_shared, (((1,), (1,)), ((), ())), preferred_element_type=jnp.float32
    )
    grad_shared_full = lax.dot_general(
        normed_low, shared_grad_low, (((0,), (0,)), ((), ())), preferred_element_type=jnp.float32
    )
    grad_gain_in = jnp.sum(grad_normed * residual_in * scale_in, axis=0)
    weighted = jnp.sum(grad_normed * norm_gain * residual_in, axis=-1, keepdims=True)
    grad_hidden = (
        out_grad.astype(jnp.float32)
        + scale_in * norm_gain * grad_normed
        - residual_in * scale_in**3 * weighted / model_width
    ).astype(jnp.bfloat16)
    grad_proj_zx, grad_proj_step, grad_proj_out = (
        lax.psum_scatter(
            grad_zx_full.astype(jnp.bfloat16), "dp", scatter_dimension=0, tiled=True
        ).astype(jnp.float32),
        lax.psum_scatter(
            grad_step_full.astype(jnp.bfloat16), "dp", scatter_dimension=0, tiled=True
        ).astype(jnp.float32),
        lax.psum_scatter(
            grad_out_full.astype(jnp.bfloat16), "dp", scatter_dimension=1, tiled=True
        ).astype(jnp.float32),
    )
    grad_proj_shared = lax.psum_scatter(
        grad_shared_full, ("dp", "tensor"), scatter_dimension=0, tiled=True
    )
    grad_conv_inner, grad_step_bias, grad_decay_log, grad_skip_gain, grad_gated_gain = lax.psum(
        (grad_conv_in, grad_bias, grad_decay, grad_skip, grad_gain_mix), "dp"
    )
    grad_norm_gain, grad_conv_shared = lax.psum((grad_gain_in, grad_conv_sh), ("dp", "tensor"))
    return (
        hidden_out,
        grad_hidden,
        grad_norm_gain,
        grad_proj_zx,
        grad_proj_shared,
        grad_proj_step,
        grad_conv_inner,
        grad_conv_shared,
        grad_step_bias,
        grad_decay_log,
        grad_skip_gain,
        grad_gated_gain,
        grad_proj_out,
    )


def solution(mesh):
    return jax.shard_map(
        per_device,
        mesh=mesh,
        in_specs=(
            P(("dp", "tensor"), None),
            P(),
            P("dp", None, "tensor"),
            P(("dp", "tensor"), None),
            P("dp", "tensor"),
            P(None, "tensor"),
            P(),
            P("tensor"),
            P("tensor"),
            P("tensor"),
            P("tensor"),
            P("tensor", "dp"),
            P(("dp", "tensor"), None),
            P("dp"),
        ),
        out_specs=(
            P(("dp", "tensor"), None),
            P(("dp", "tensor"), None),
            P(),
            P("dp", None, "tensor"),
            P(("dp", "tensor"), None),
            P("dp", "tensor"),
            P(None, "tensor"),
            P(),
            P("tensor"),
            P("tensor"),
            P("tensor"),
            P("tensor"),
            P("tensor", "dp"),
        ),
        check_vma=False,
    )
```

profile of v0, /device:TPU:24, one launch (start us, length us, event | category | flops | bytes accessed | tf_op | source)
XLA Modules:
  0.0 1471.1 jit_solution(17162407354371005518)
XLA Ops:
  15.2 170.3 %all-gather.1 = bf16[128,12,256]{2,1,0:T(8,128)(2,1)S(1)} all-gather(bf16[1,12,256]{2,1,0:T(8,128)(2,1)S(1)} %bitcast.591), channel_id=1, replica_groups=mesh['dp'=32,'tensor'=4] {'dp','tensor'}, dimensions={0}, use_global_device_ids=true | all-gather | bytes 792576 | tf_op jit(solution)/shard_map/all_gather | solution.py:123
  186.4 79.1 %all-gather = bf16[32,48,12]{1,2,0:T(8,128)(2,1)S(1)} all-gather(bf16[1,48,12]{1,2,0:T(8,128)(2,1)S(1)} %bitcast.593), channel_id=1, replica_groups=mesh['dp'=32,'tensor'=4] {'dp'}, dimensions={0}, use_global_device_ids=true | all-gather | bytes 38016 | tf_op jit(solution)/shard_map/all_gather | solution.py:120
  280.2 7.1 fusion.146
  307.3 122.7 %while.82 = (s32[]{:T(128)}, f32[12,128,64]{1,2,0:T(8,128)S(1)}, f32[4,256,12,64]{1,3,2,0:T(8,128)}, f32[4,128,256]{1,2,0:T(8,128)}, pred[4,12,256,256]{3,2,1,0:...) while((s32[]{:T(128)}, f32[12,128,64]{1,2,0:T(8,128)S(1)}, ...), condition=%wide.region_4.5_spmd.clone, body=%wide.region_1.4_spmd.clone.sunk | while | flops 1317000704 | bytes 23156852 | solution.py:90
  324.5 5.9 fusion.253
  355.0 5.9 fusion.253
  385.6 6.2 fusion.253
  416.5 5.9 fusion.253
  449.6 7.2 psum.63
  456.9 10.8 multiply_reduce_fusion
  467.6 7.2 psum.64
  474.9 7.1 fusion.163
  495.2 223.0 %while.83 = (s32[]{:T(128)}, f32[12]{0:T(128)S(1)}, f32[12,128,64]{1,2,0:T(8,128)S(1)}, f32[4,256,12,64]{1,0,3,2:T(4,128)}, f32[4,256,128]{2,1,0:T(8,128)}, /*in...) while((s32[]{:T(128)}, f32[12]{0:T(128)S(1)}, ...), condition=%wide.region_22.23_spmd.clone, body=%wide.region_10.22_spmd.clone.sunk | while | flops 2628679680 | bytes 31450640 | solution.py:90
  500.0 6.5 fusion.271
  523.5 17.9 %dynamic_update_slice.267 = f32[4,256,12,64]{1,0,3,2:T(4,128)} dynamic-update-slice(f32[4,256,12,64]{1,0,3,2:T(4,128)} %get-tuple-element.2507, f32[1,256,12,64]{1,0,3,2:T(1,128)S(1)} %copy.304, s32[]{:T(128)S(6)} %sub.241, s32[]{:T(128)} %constant.206.clone.1..sunk.1, s32[]{:T(128)} %constant.206.clone.1..sunk.1, s32[]{:T(128)} %constant.206.clone.1..sunk.1) | dynamic-update-slice | bytes 1572868 | tf_op jit(solution)/shard_map/transpose(jvp())/while/body/jit(dynamic_update_index_in_dim)/dynamic_update_slice | solution.py:90
  555.6 6.5 fusion.271
  579.2 17.9 %dynamic_update_slice.267 = f32[4,256,12,64]{1,0,3,2:T(4,128)} dynamic-update-slice(f32[4,256,12,64]{1,0,3,2:T(4,128)} %get-tuple-element.2507, f32[1,256,12,64]{1,0,3,2:T(1,128)S(1)} %copy.304, s32[]{:T(128)S(6)} %sub.241, s32[]{:T(128)} %constant.206.clone.1..sunk.1, s32[]{:T(128)} %constant.206.clone.1..sunk.1, s32[]{:T(128)} %constant.206.clone.1..sunk.1) | dynamic-update-slice | bytes 1572868 | tf_op jit(solution)/shard_map/transpose(jvp())/while/body/jit(dynamic_update_index_in_dim)/dynamic_update_slice | solution.py:90
  611.3 6.5 fusion.271
  634.8 17.9 %dynamic_update_slice.267 = f32[4,256,12,64]{1,0,3,2:T(4,128)} dynamic-update-slice(f32[4,256,12,64]{1,0,3,2:T(4,128)} %get-tuple-element.2507, f32[1,256,12,64]{1,0,3,2:T(1,128)S(1)} %copy.304, s32[]{:T(128)S(6)} %sub.241, s32[]{:T(128)} %constant.206.clone.1..sunk.1, s32[]{:T(128)} %constant.206.clone.1..sunk.1, s32[]{:T(128)} %constant.206.clone.1..sunk.1) | dynamic-update-slice | bytes 1572868 | tf_op jit(solution)/shard_map/transpose(jvp())/while/body/jit(dynamic_update_index_in_dim)/dynamic_update_slice | solution.py:90
  666.9 6.5 fusion.271
  690.4 17.9 %dynamic_update_slice.267 = f32[4,256,12,64]{1,0,3,2:T(4,128)} dynamic-update-slice(f32[4,256,12,64]{1,0,3,2:T(4,128)} %get-tuple-element.2507, f32[1,256,12,64]{1,0,3,2:T(1,128)S(1)} %copy.304, s32[]{:T(128)S(6)} %sub.241, s32[]{:T(128)} %constant.206.clone.1..sunk.1, s32[]{:T(128)} %constant.206.clone.1..sunk.1, s32[]{:T(128)} %constant.206.clone.1..sunk.1) | dynamic-update-slice | bytes 1572868 | tf_op jit(solution)/shard_map/transpose(jvp())/while/body/jit(dynamic_update_index_in_dim)/dynamic_update_slice | solution.py:90
  718.3 5.7 multiply_reduce_fusion.10
  728.7 7.1 convolution_convert_fusion.2
  743.8 9.4 multiply_reduce_fusion.4
  756.6 7.0 convolution_convert_fusion
  765.4 7.2 fusion.149
  778.2 5.9 convolution_convert_fusion.1
  786.6 313.7 %fusion.2 = f32[16,256]{1,0:T(8,128)S(1)} fusion(f32[1536,256]{1,0:T(8,128)S(1)} %fusion.171), kind=kCustom, calls=%all-reduce-scatter | all-reduce-scatter fusion | flops 524289 | bytes 1589248
  1100.3 42.5 %collective-permute-start = (f32[16,256]{1,0:T(8,128)S(1)}, f32[16,256]{1,0:T(8,128)S(1)}, u32[]{:S(2)}, u32[]{:S(2)}) collective-permute-start(f32[16,256]{1,0:T(8,128)S(1)} %fusion.2), channel_id=1, source_target_pairs={{0,1},{1,2},{2,3},{3,4},{4,5},{5,6},{6,7},{7,8},{8,9},{9,10},{10,1... | collective-permute-start | bytes 49160
  1144.1 5.4 collective-permute-start.1
  1217.7 157.0 %all-reduce.28 = (f32[5,768]{1,0:T(8,128)}, f32[12]{0:T(128)}, f32[12]{0:T(128)}, f32[12]{0:T(128)}, f32[768]{0:T(1024)}) all-reduce(f32[5,768]{1,0:T(8,128)S(1)} %pad_add_fusion.6, f32[12]{0:T(128)} %get-tuple-element.1833, f32[12]{0:T(128)S(1)} %exponential_multiply_fusion, ...), channel_id=1, replica_groups=mesh['dp'=32,'tensor'=4] {'dp'}, use_global_device_ids=true, to_apply=%region_36.37 | all-reduce | flops 4644 | bytes 37152 | tf_op jit(solution)/shard_map/psum | solution.py:226
  1386.1 74.9 %all-reduce.27 = (f32[1536]{0:T(1024)}, f32[5,256]{1,0:T(8,128)}) all-reduce(f32[1536]{0:T(1024)S(1)} %get-tuple-element.1678, f32[5,256]{1,0:T(8,128)S(1)} %pad_add_fusion.7), channel_id=1, replica_groups=mesh['dp'=32,'tensor'=4] {'dp','tensor'}, use_global_device_ids=true, to_apply=%region_27.28 | all-reduce | flops 2816 | bytes 22528 | tf_op jit(solution)/shard_map/psum | solution.py:229
  (624 shorter events, 402.4 us)
Async XLA Ops:
  7.2 260.4 %all-gather.7.cloned.1.call-start = ((), (), s32[]{:S(2)}) async-start(), calls=%async_computation.6 | async-start | bytes 3932160 | tf_op jit(solution)/shard_map/all_gather | solution.py:124
  11.5 268.6 %all-gather.9.cloned.1.call-start = ((), (), s32[]{:S(2)}) async-start(), calls=%async_computation.7 | async-start | bytes 4866048 | tf_op jit(solution)/shard_map/all_gather | solution.py:119
  12.3 444.5 %all-gather.11.cloned.1.call-start = ((), (), s32[]{:S(2)}) async-start(), calls=%async_computation.8 | async-start | bytes 2433024 | tf_op jit(solution)/shard_map/all_gather | solution.py:121
  13.0 443.8 %all-gather.13.cloned.1.call-start = ((), (), s32[]{:S(2)}) async-start(), calls=%async_computation.10 | async-start | bytes 3932160 | tf_op jit(solution)/shard_map/all_gather | solution.py:125
  13.6 770.6 %reduce-scatter.15.cloned.1.call-start = ((), (), s32[]{:S(2)}) async-start(), calls=%async_computation.12 | async-start | bytes 1310720 | tf_op jit(solution)/shard_map/reduce_scatter | solution.py:196
  726.2 648.5 %reduce-scatter.21.cloned.1.call-start = ((), (), s32[]{:S(2)}) async-start(), calls=%async_computation.15 | async-start | bytes 405504
  728.7 651.8 %reduce-scatter.19.cloned.1.call-start = ((), (), s32[]{:S(2)}) async-start(), calls=%async_computation.14 | async-start | bytes 2433024 | tf_op jit(solution)/shard_map/reduce_scatter | solution.py:219
  735.8 646.1 %reduce-scatter.17.cloned.1.call-start = ((), (), s32[]{:S(2)}) async-start(), calls=%async_computation.13 | async-start | bytes 4866048 | tf_op jit(solution)/shard_map/reduce_scatter | solution.py:213
  763.6 620.1 %reduce-scatter.13.cloned.1.call-start = ((), (), s32[]{:S(2)}) async-start(), calls=%async_computation.11 | async-start | bytes 7864320 | tf_op jit(solution)/shard_map/reduce_scatter | solution.py:195
  776.3 684.7 %reduce-scatter.11.cloned.1.call-start = ((), (), s32[]{:S(2)}) async-start(), calls=%async_computation.9 | async-start | bytes 3932160 | tf_op jit(solution)/shard_map/reduce_scatter | solution.py:146
  1100.3 59.2 %collective-permute-start = (f32[16,256]{1,0:T(8,128)S(1)}, f32[16,256]{1,0:T(8,128)S(1)}, u32[]{:S(2)}, u32[]{:S(2)}) collective-permute-start(f32[16,256]{1,0:T(8,128)S(1)} %fusion.2), channel_id=1, source_target_pairs={{0,1},{1,2},{2,3},{3,4},{4,5},{5,6},{6,7},{7,8},{8,9},{9,10},{10,1... | collective-permute-start | bytes 49160
  1142.8 13.1 collective-permute-start.31
  1144.1 18.3 %collective-permute-start.1 = (f32[16,256]{1,0:T(8,128)S(1)}, f32[16,256]{1,0:T(8,128)S(1)}, u32[]{:S(2)}, u32[]{:S(2)}) collective-permute-start(f32[16,256]{1,0:T(8,128)S(1)} %fusion.2), channel_id=1, source_target_pairs={{0,2},{1,3},{2,4},{3,5},{4,6},{5,7},{6,8},{7,9},{8,10},{9,11},{10,... | collective-permute-start | bytes 49160
  1149.5 14.8 %collective-permute-start.10 = (f32[16,256]{1,0:T(8,128)S(1)}, f32[16,256]{1,0:T(8,128)S(1)}, u32[]{:S(2)}, u32[]{:S(2)}) collective-permute-start(f32[16,256]{1,0:T(8,128)S(1)} %fusion.2), channel_id=1, source_target_pairs={{0,11},{1,12},{2,13},{3,14},{4,15},{5,16},{6,17},{7,18},{8,19},{9,... | collective-permute-start | bytes 49160
  1152.1 14.2 collective-permute-start.11
  1155.9 12.3 collective-permute-start.12
  1159.5 10.7 collective-permute-start.13
  1166.3 11.4 collective-permute-start.16
  1168.2 11.4 collective-permute-start.17
  1170.2 11.3 collective-permute-start.18
  1172.1 11.3 collective-permute-start.19
  1174.1 11.3 collective-permute-start.2
  1191.5 10.8 collective-permute-start.27
  1196.1 11.0 collective-permute-start.29
  1198.0 12.2 collective-permute-start.3
  1200.0 12.2 collective-permute-start.30
  1202.3 11.8 collective-permute-start.4
  1204.4 171.7 %collective-permute-start.5 = (f32[16,256]{1,0:T(8,128)S(1)}, f32[16,256]{1,0:T(8,128)S(1)}, u32[]{:S(2)}, u32[]{:S(2)}) collective-permute-start(f32[16,256]{1,0:T(8,128)S(1)} %fusion.2), channel_id=1, source_target_pairs={{0,6},{1,7},{2,8},{3,9},{4,10},{5,11},{6,12},{7,13},{8,14},{9,15},... | collective-permute-start | bytes 49160
  1207.1 169.0 %collective-permute-start.6 = (f32[16,256]{1,0:T(8,128)S(1)}, f32[16,256]{1,0:T(8,128)S(1)}, u32[]{:S(2)}, u32[]{:S(2)}) collective-permute-start(f32[16,256]{1,0:T(8,128)S(1)} %fusion.2), channel_id=1, source_target_pairs={{0,7},{1,8},{2,9},{3,10},{4,11},{5,12},{6,13},{7,14},{8,15},{9,16}... | collective-permute-start | bytes 49160
  1210.2 165.9 %collective-permute-start.7 = (f32[16,256]{1,0:T(8,128)S(1)}, f32[16,256]{1,0:T(8,128)S(1)}, u32[]{:S(2)}, u32[]{:S(2)}) collective-permute-start(f32[16,256]{1,0:T(8,128)S(1)} %fusion.2), channel_id=1, source_target_pairs={{0,8},{1,9},{2,10},{3,11},{4,12},{5,13},{6,14},{7,15},{8,16},{9,17... | collective-permute-start | bytes 49160
  1212.2 164.0 %collective-permute-start.8 = (f32[16,256]{1,0:T(8,128)S(1)}, f32[16,256]{1,0:T(8,128)S(1)}, u32[]{:S(2)}, u32[]{:S(2)}) collective-permute-start(f32[16,256]{1,0:T(8,128)S(1)} %fusion.2), channel_id=1, source_target_pairs={{0,9},{1,10},{2,11},{3,12},{4,13},{5,14},{6,15},{7,16},{8,17},{9,1... | collective-permute-start | bytes 49160
  1214.1 162.0 %collective-permute-start.9 = (f32[16,256]{1,0:T(8,128)S(1)}, f32[16,256]{1,0:T(8,128)S(1)}, u32[]{:S(2)}, u32[]{:S(2)}) collective-permute-start(f32[16,256]{1,0:T(8,128)S(1)} %fusion.2), channel_id=1, source_target_pairs={{0,10},{1,11},{2,12},{3,13},{4,14},{5,15},{6,16},{7,17},{8,18},{9,... | collective-permute-start | bytes 49160
  (83 other events, 6177.6 us)
Sparse Core Ops, SparseCore 0:
  11.7 35.8 all-gather.6
  49.8 152.1 all-gather.8
  203.6 154.0 all-gather.10
  359.2 39.9 all-gather.12
  726.3 43.8 reduce-scatter.14
  772.5 144.9 reduce-scatter.20
  919.9 159.9 reduce-scatter.18
  1082.3 168.2 reduce-scatter.16
  1253.3 76.4 reduce-scatter.12
  1332.5 44.5 reduce-scatter.10
where the time goes:
time: 1490 us; the launch traced here: 1470 us
  blocking collectives  810 us (54%)
  local copies, waits for them, and re-layouts  222 us (15%)
  matrix products  184 us (12%)
  other arithmetic  116 us (8%)
  starting transfers between devices  115 us (8%)
  between operations  15.9 us (1%)
    unnamed x1, blocking collectives  314 us
    all_gather x1, blocking collectives, per_device(): lax.all_gather(proj_shared, ('dp', 'tensor'), axis=0, tiled=True)  170 us
    psum x1, blocking collectives, per_device(): lax.psum((grad_conv_in, grad_bias, grad_decay, grad_skip, grad_gain_mix),...  157 us
    unnamed x33, starting transfers between devices  114 us
    dynamic_update_slice x52, local copies, waits for them, and re-layouts, block_mixer(): lax.scan(advance, initial, (inner_blocks, write_blocks, read_blocks, step...  100 us
    all_gather x1, blocking collectives, per_device(): lax.all_gather(proj_step, 'dp', axis=0, tiled=True)  79.1 us
    psum x1, blocking collectives, per_device(): lax.psum((grad_gain_in, grad_conv_sh), ('dp', 'tensor'))  74.9 us
    dot_general x12, matrix products, advance(): within = jnp.einsum('hts,shp->thp', weights, inner_here, precision=HIGH)  65.7 us
  transfers between devices with their start and end apart: 42, of which 4 were waited for; matrix products, arithmetic and copies ran while one was open for 38% of the time, Pallas kernels for 0%

commit v1 on v0

v1 whole, which is shorter than its diff:
```python
from functools import partial

import jax
import jax.numpy as jnp
from jax import lax
from jax.sharding import Mesh
from jax.sharding import PartitionSpec as P

SPAN = 256
EPS = 1e-05
HIGH = lax.Precision.HIGHEST
F32 = jnp.float32
BF16 = jnp.bfloat16
DP = ("y", "x", "zl")
TENSOR = ("zh", "c")
SIZES = {"y": 4, "x": 4, "zl": 2, "zh": 2, "c": 2}


def shift(value, axis, by):
    n = SIZES[axis]
    return lax.ppermute(value, axis, [(i, (i - by) % n) for i in range(n)])


def swap(value, axis):
    return shift(value, axis, 1)


def ordered_pair(own, other, axis):
    first = lax.axis_index(axis) == 0
    return jnp.stack([jnp.where(first, own, other), jnp.where(first, other, own)], 0)


def gather_pair(value, axis):
    return ordered_pair(value, swap(value, axis), axis)


def gather_ring(value, axis):
    parts = [value, shift(value, axis, 1), shift(value, axis, 2), shift(value, axis, -1)]
    turned = jnp.stack(parts + parts[:3], 0)
    start = (4 - lax.axis_index(axis)) % 4
    return lax.dynamic_slice_in_dim(turned, start, 4, 0)


def gather_dp(value):
    pair = gather_pair(value, "zl")
    rows = gather_ring(pair, "x")
    full = gather_ring(rows, "y")
    return full.reshape((32 * value.shape[0],) + value.shape[1:])


def scatter_ring(value, axis):
    me = lax.axis_index(axis)

    def entry(by):
        return lax.dynamic_index_in_dim(value, (me + by) % 4, 0, keepdims=False)

    ahead = shift(entry(-1), axis, 1)
    behind = shift(entry(1), axis, -1)
    across = shift(entry(2), axis, 2)
    return (entry(0).astype(F32) + across.astype(F32)) + (ahead.astype(F32) + behind.astype(F32))


def scatter_pair(value, axis):
    me = lax.axis_index(axis)
    keep = lax.dynamic_index_in_dim(value, me, 0, keepdims=False)
    give = lax.dynamic_index_in_dim(value, 1 - me, 0, keepdims=False)
    return keep.astype(F32) + swap(give, axis).astype(F32)


def scatter_dp(value):
    width = value.shape[1]
    blocks = value.reshape(4, 4, 2, 48, width)
    mine = scatter_ring(blocks, "y").astype(BF16)
    mine = scatter_ring(mine, "x").astype(BF16)
    return scatter_pair(mine, "zl")


def sum_ring(value, axis):
    ahead, behind, across = shift(value, axis, 1), shift(value, axis, -1), shift(value, axis, 2)
    return (value + across) + (ahead + behind)


def sum_pair(value, axis):
    return value + swap(value, axis)


def gather_tokens(value):
    far = swap(value, "zh")
    near_pair = gather_pair(value, "c")
    far_pair = gather_pair(far, "c")
    both = ordered_pair(near_pair, far_pair, "zh")
    return both.reshape((4 * value.shape[0],) + value.shape[1:])


def scatter_tensor(value):
    by_zh = value.reshape((2, 2) + value.shape[1:])
    half = scatter_pair(jnp.swapaxes(by_zh, 0, 1), "c").astype(BF16)
    return scatter_pair(half, "zh")


def causal_conv(values, conv_taps, segment_ids):
    length = values.shape[0]
    padded = jnp.concatenate([jnp.zeros((3, values.shape[1]), values.dtype), values], 0)
    seg_pad = jnp.concatenate([jnp.full((3,), -1, jnp.int32), segment_ids], 0)
    summed = conv_taps[4] + jnp.zeros_like(values)
    for offset in range(4):
        same_doc = (seg_pad[offset : offset + length] == segment_ids)[:, None]
        summed = summed + conv_taps[offset] * jnp.where(
            same_doc, padded[offset : offset + length], 0.0
        )
    return jax.nn.silu(summed)


def block_mixer(
    inner_pre,
    shared_pre,
    step_pre,
    conv_inner,
    conv_shared,
    step_bias,
    decay_log,
    skip_gain,
    segment_ids=None,
    block_len=None,
):
    inner_conv = causal_conv(inner_pre, conv_inner, segment_ids)
    shared_conv = causal_conv(shared_pre, conv_shared, segment_ids)
    length, inner_width = inner_conv.shape
    head_count = step_bias.shape[0]
    head_size = inner_width // head_count
    states = shared_conv.shape[1] // 2
    blocks = length // block_len
    step_sizes = jax.nn.softplus(step_pre + step_bias)
    log_decay = -step_sizes * jnp.exp(decay_log)
    inner_blocks = inner_conv.reshape(blocks, block_len, head_count, head_size)
    write_blocks = shared_conv[:, :states].reshape(blocks, block_len, states)
    read_blocks = shared_conv[:, states:].reshape(blocks, block_len, states)
    step_blocks = step_sizes.reshape(blocks, block_len, head_count)
    log_blocks = log_decay.reshape(blocks, block_len, head_count)
    doc_blocks = segment_ids.reshape(blocks, block_len)
    doc_before = jnp.concatenate([jnp.full((1,), -1, jnp.int32), doc_blocks[:-1, -1]], 0)
    places = jnp.arange(block_len)
    lower_tri = places[:, None] >= places[None, :]

    def advance(carried, operands):
        inner_here, write_here, read_here, step_here, log_here, doc_here, prior_doc = operands
        cumulative = jnp.cumsum(log_here, axis=0)
        allowed = lower_tri & (doc_here[:, None] == doc_here[None, :])
        inner_prod = jnp.dot(read_here, write_here.T, precision=HIGH)
        spread = jnp.where(
            allowed[None], cumulative.T[:, :, None] - cumulative.T[:, None, :], -jnp.inf
        )
        weights = jnp.exp(spread) * inner_prod[None] * step_here.T[:, None, :]
        within = jnp.einsum("hts,shp->thp", weights, inner_here, precision=HIGH)
        enters = jnp.where((doc_here == prior_doc)[:, None], jnp.exp(cumulative), 0.0)
        from_state = (
            jnp.einsum("tn,hnp->thp", read_here, carried, precision=HIGH) * enters[:, :, None]
        )
        result = within + from_state + inner_here * skip_gain[None, :, None]
        to_end = (
            jnp.where(
                (doc_here == doc_here[-1])[:, None],
                jnp.exp(cumulative[-1][None, :] - cumulative),
                0.0,
            )
            * step_here
        )
        carry_keep = jnp.where(doc_here[-1] == prior_doc, jnp.exp(cumulative[-1]), 0.0)
        updated = carried * carry_keep[:, None, None] + jnp.einsum(
            "sn,shp->hnp", write_here, inner_here * to_end[:, :, None], precision=HIGH
        )
        return (updated, result)

    initial = jnp.zeros((head_count, states, head_size), F32)
    unused, outputs = lax.scan(
        advance,
        initial,
        (inner_blocks, write_blocks, read_blocks, step_blocks, log_blocks, doc_blocks, doc_before),
    )
    return outputs.reshape(length, inner_width)


def per_device(
    hidden_in,
    norm_gain,
    proj_zx,
    proj_shared,
    proj_step,
    conv_inner,
    conv_shared,
    step_bias,
    decay_log,
    skip_gain,
    gated_gain,
    proj_out,
    out_grad,
    segments,
):
    model_width = hidden_in.shape[1]
    width = proj_zx.shape[2]
    inner_width = width * 4
    heads = step_bias.shape[0]
    residual_in = hidden_in.astype(F32)
    scale_in = lax.rsqrt(jnp.mean(residual_in * residual_in, axis=-1, keepdims=True) + EPS)
    normed_low = (residual_in * scale_in * norm_gain).astype(BF16)

    shared_rows = gather_tokens(proj_shared)
    first_rows = jnp.concatenate(
        [proj_zx[:, 1, :], shared_rows, jnp.pad(proj_step, ((0, 0), (0, 128 - heads)))], 1
    )
    first_full = gather_dp(first_rows)
    tokens = gather_tokens(normed_low)
    second_rows = jnp.concatenate([proj_zx[:, 0, :], proj_out.T], 1)
    second_rows, first_done = lax.optimization_barrier((second_rows, first_full))
    second_full = gather_dp(second_rows)
    out_grad_late, tokens = lax.optimization_barrier((out_grad, tokens))
    grad_rows = gather_tokens(out_grad_late)

    first_pre = jnp.dot(tokens, first_full, preferred_element_type=F32)
    inner_pre = first_pre[:, :width]
    shared_pre = first_pre[:, width : width + 256]
    step_pre = first_pre[:, width + 256 : width + 256 + heads]
    mixer_fn = partial(block_mixer, segment_ids=segments, block_len=SPAN)
    scanned, mixer_back = jax.vjp(
        mixer_fn,
        inner_pre,
        shared_pre,
        step_pre,
        conv_inner,
        conv_shared,
        step_bias,
        decay_log,
        skip_gain,
    )
    gate_full = second_full[:, :width]
    out_full = second_full[:, width:]
    gate_pre = jnp.dot(tokens, gate_full, preferred_element_type=F32)
    grad_mixed = jnp.dot(grad_rows, out_full, preferred_element_type=F32)
    gate_sig = jax.nn.sigmoid(gate_pre)
    gate_act = gate_pre * gate_sig
    gated = scanned * gate_act
    sums = jnp.stack(
        [jnp.sum(gated * gated, axis=-1), jnp.sum(grad_mixed * gated_gain * gated, axis=-1)], 0
    )
    sums = sum_pair(sum_pair(sums, "c"), "zh")
    scale_mix = lax.rsqrt(sums[0] / inner_width + EPS)[:, None]
    norm_dot = (sums[1] / inner_width)[:, None]
    gated_scaled = gated * scale_mix
    mixed_low = (gated_scaled * gated_gain).astype(BF16)
    grad_gain_mix = jnp.sum(grad_mixed * gated_scaled, axis=0)
    grad_gated = scale_mix * gated_gain * grad_mixed - gated * scale_mix**3 * norm_dot
    grad_scanned = grad_gated * gate_act
    grad_gate = grad_gated * scanned * gate_sig * (1 + gate_pre * (1 - gate_sig))
    gate_grad_low = grad_gate.astype(BF16)

    mixed_sum = scatter_tensor(
        lax.dot_general(
            mixed_low, out_full, (((1,), (1,)), ((), ())), preferred_element_type=F32
        )
        .astype(BF16)
        .reshape(4, -1, model_width)
    )
    hidden_out = (residual_in + mixed_sum).astype(BF16)
    to_model = (((0,), (0,)), ((), ()))
    second_grad = jnp.concatenate(
        [
            lax.dot_general(tokens, gate_grad_low, to_model, preferred_element_type=F32),
            lax.dot_general(grad_rows, mixed_low, to_model, preferred_element_type=F32),
        ],
        1,
    ).astype(BF16)
    second_mine = scatter_dp(second_grad)
    grad_proj_gate = second_mine[:, :width]
    grad_proj_out = second_mine[:, width:].T

    (
        grad_inner,
        grad_shared,
        grad_step,
        grad_conv_in,
        grad_conv_sh,
        grad_bias,
        grad_decay,
        grad_skip,
    ) = mixer_back(grad_scanned)
    first_grad_low = jnp.concatenate(
        [grad_inner, grad_shared, jnp.pad(grad_step, ((0, 0), (0, 128 - heads)))], 1
    ).astype(BF16)
    to_tokens = (((1,), (1,)), ((), ()))
    grad_tokens = lax.dot_general(
        gate_grad_low, gate_full, to_tokens, preferred_element_type=F32
    ) + lax.dot_general(first_grad_low, first_full, to_tokens, preferred_element_type=F32)
    grad_gain_in = jnp.sum(grad_tokens * tokens.astype(F32), axis=0) / norm_gain
    grad_normed = scatter_tensor(grad_tokens.astype(BF16).reshape(4, -1, model_width))
    weighted = jnp.sum(grad_normed * norm_gain * residual_in, axis=-1, keepdims=True)
    grad_hidden = (
        out_grad.astype(F32)
        + scale_in * norm_gain * grad_normed
        - residual_in * scale_in**3 * weighted / model_width
    ).astype(BF16)

    first_grad = lax.dot_general(tokens, first_grad_low, to_model, preferred_element_type=F32).astype(BF16)
    shared_parts = first_grad[:, width : width + 256].reshape(32, 4, 12, 256).swapaxes(0, 1)
    shared_part = scatter_tensor(shared_parts).astype(BF16).reshape(1536, 64)
    first_pack = jnp.concatenate(
        [first_grad[:, :width], shared_part, first_grad[:, width + 256 : width + 256 + 64]], 1
    )
    first_mine = scatter_dp(first_pack)
    grad_proj_inner = first_mine[:, :width]
    grad_proj_shared = first_mine[:, width : width + 64].reshape(12, 256)
    grad_proj_step = first_mine[:, width + 64 : width + 64 + heads]
    grad_proj_zx = jnp.stack([grad_proj_gate, grad_proj_inner], 1)

    everywhere = jnp.concatenate([grad_gain_in, grad_conv_sh.reshape(-1)])
    everywhere = sum_pair(sum_pair(everywhere, "c"), "zh")
    small = jnp.concatenate(
        [everywhere, grad_conv_in.reshape(-1), grad_gain_mix, grad_bias, grad_decay, grad_skip]
    )
    count = small.shape[0]
    small = jnp.pad(small, (0, 8192 - count)).reshape(8, 1024)
    small = sum_pair(sum_ring(sum_ring(small, "y"), "x"), "zl").reshape(-1)
    cuts = [model_width, 5 * 256, 5 * width, width, heads, heads, heads]
    parts, place = [], 0
    for size in cuts:
        parts.append(small[place : place + size])
        place += size
    return (
        hidden_out,
        grad_hidden,
        parts[0],
        grad_proj_zx,
        grad_proj_shared,
        grad_proj_step,
        parts[2].reshape(5, width),
        parts[1].reshape(5, 256),
        parts[4],
        parts[5],
        parts[6],
        parts[3],
        grad_proj_out,
    )


def solution(mesh):
    fine = Mesh(mesh.devices.reshape(4, 4, 2, 2, 2), DP + TENSOR)
    both = DP + TENSOR
    return jax.shard_map(
        per_device,
        mesh=fine,
        in_specs=(
            P(both, None),
            P(),
            P(DP, None, TENSOR),
            P(both, None),
            P(DP, TENSOR),
            P(None, TENSOR),
            P(),
            P(TENSOR),
            P(TENSOR),
            P(TENSOR),
            P(TENSOR),
            P(TENSOR, DP),
            P(both, None),
            P(DP),
        ),
        out_specs=(
            P(both, None),
            P(both, None),
            P(),
            P(DP, None, TENSOR),
            P(both, None),
            P(DP, TENSOR),
            P(None, TENSOR),
            P(),
            P(TENSOR),
            P(TENSOR),
            P(TENSOR),
            P(TENSOR),
            P(TENSOR, DP),
        ),
        check_vma=False,
    )
```

time: 1490 us -> 914 us (0.61)
  blocking collectives: 810 us -> 0 us
  waiting for transfers between devices: 2.42 us -> 172 us
  local copies, waits for them, and re-layouts: 222 us -> 336 us
  starting transfers between devices: 115 us -> 62.9 us
  other arithmetic: 116 us -> 148 us
    unnamed x1 -> x0, blocking collectives: 314 us -> none
    all_gather x2 -> x0, blocking collectives: 249 us -> none  [the longest x1 170 us: per_device(): lax.all_gather(proj_shared, ('dp', 'tensor'), axis=0, tiled=True)]
    psum x4 -> x0, blocking collectives: 246 us -> none  [the longest x1 157 us: per_device(): lax.psum((grad_conv_in, grad_bias, grad_decay, grad_skip, grad_gain_mix),...]
    ppermute x0 -> x54, waiting for transfers between devices: none -> 172 us  [shift(): return lax.ppermute(value, axis, [(i, (i - by) % n) for i in range(n)])]
    unnamed x33 -> x0, starting transfers between devices: 114 us -> none
    dynamic_update_slice x52 -> x44, local copies, waits for them, and re-layouts: 100 us -> 170 us  [block_mixer(): lax.scan(advance, initial, (inner_blocks, write_blocks, read_blocks, step...]
    ppermute x0 -> x54, starting transfers between devices: none -> 62.9 us  [shift(): return lax.ppermute(value, axis, [(i, (i - by) % n) for i in range(n)])]
    unnamed x164 -> x235, local copies, waits for them, and re-layouts: 29.2 us -> 47.9 us
  transfers between devices with their start and end apart: 42 -> 54, of which waited for: 4 -> 23; matrix products, arithmetic and copies ran while one was open for 38% -> 38% of each run, Pallas kernels for 0% -> 0%
where the time goes in v1:
time: 914 us; the launch traced here: 898 us
  local copies, waits for them, and re-layouts  336 us (37%)
  waiting for transfers between devices  172 us (19%)
  matrix products  171 us (19%)
  other arithmetic  148 us (16%)
  starting transfers between devices  62.9 us (7%)
    ppermute x54, waiting for transfers between devices, shift(): return lax.ppermute(value, axis, [(i, (i - by) % n) for i in range(n)])  172 us
    dynamic_update_slice x44, local copies, waits for them, and re-layouts, block_mixer(): lax.scan(advance, initial, (inner_blocks, write_blocks, read_blocks, step...  170 us
    ppermute x54, starting transfers between devices, shift(): return lax.ppermute(value, axis, [(i, (i - by) % n) for i in range(n)])  62.9 us
    dot_general x12, matrix products, advance(): within = jnp.einsum('hts,shp->thp', weights, inner_here, precision=HIGH)  62 us
    unnamed x235, local copies, waits for them, and re-layouts  47.9 us
    dynamic_update_slice x24, other arithmetic, block_mixer(): lax.scan(advance, initial, (inner_blocks, write_blocks, read_blocks, step...  40.5 us
    dot_general x12, matrix products, advance(): jnp.einsum('sn,shp->hnp', write_here, inner_here * to_end[:, :, None], pr...  27 us
    dynamic_slice x16, local copies, waits for them, and re-layouts, block_mixer(): lax.scan(advance, initial, (inner_blocks, write_blocks, read_blocks, step...  20.9 us
  transfers between devices with their start and end apart: 54, of which 23 were waited for; matrix products, arithmetic and copies ran while one was open for 38% of the time, Pallas kernels for 0%

profile of v1, /device:TPU:24, one launch (start us, length us, event | category | flops | bytes accessed | tf_op | source)
XLA Modules:
  0.0 898.2 jit_solution(9221175793933558211)
XLA Ops:
  20.2 8.1 collective-permute-done.7
  40.0 35.0 %collective-permute-done.10 = bf16[4,2,48,1152]{3,2,1,0:T(8,128)(2,1)S(1)} collective-permute-done((bf16[4,2,48,1152]{3,2,1,0:T(8,128)(2,1)S(1)}, bf16[4,2,48,1152]{3,2,1,0:T(8,128)(2,1)S(1)}, u32[]{:S(2)}, u32[]{:S(2)}) %collective-permute-start.10) | collective-permute-done | bytes 884768 | tf_op jit(solution)/shard_map/ppermute | solution.py:21
  143.8 199.5 %while.82 = (s32[]{:T(128)}, f32[12,128,64]{1,2,0:T(8,128)S(1)}, f32[4,256,12,64]{1,0,3,2:T(4,128)}, f32[4,128,256]{1,2,0:T(8,128)}, pred[4,12,256,256]{3,2,1,0:...) while((s32[]{:T(128)}, f32[12,128,64]{1,2,0:T(8,128)S(1)}, ...), condition=%wide.region_4.5_spmd.clone, body=%wide.region_1.4_spmd.clone.sunk | while | flops 1317000704 | bytes 26281080 | solution.py:175
  163.6 17.9 %dynamic_update_slice.262 = f32[4,256,12,64]{1,0,3,2:T(4,128)} dynamic-update-slice(f32[4,256,12,64]{1,0,3,2:T(4,128)} %get-tuple-element.2368, f32[1,256,12,64]{1,0,3,2:T(1,128)S(1)} %copy.287, s32[]{:T(128)S(6)} %copy.359, s32[]{:T(128)} %constant.380.clone.1..sunk, s32[]{:T(128)} %constant.380.clone.1..sunk, s32[]{:T(128)} %constant.380.clone.1..sunk) | dynamic-update-slice | bytes 1572868 | tf_op jit(solution)/shard_map/jvp()/while/body/jit(dynamic_update_index_in_dim)/dynamic_update_slice | solution.py:175
  207.4 5.0 fusion.272
  213.3 17.9 %dynamic_update_slice.262 = f32[4,256,12,64]{1,0,3,2:T(4,128)} dynamic-update-slice(f32[4,256,12,64]{1,0,3,2:T(4,128)} %get-tuple-element.2368, f32[1,256,12,64]{1,0,3,2:T(1,128)S(1)} %copy.287, s32[]{:T(128)S(6)} %copy.359, s32[]{:T(128)} %constant.380.clone.1..sunk, s32[]{:T(128)} %constant.380.clone.1..sunk, s32[]{:T(128)} %constant.380.clone.1..sunk) | dynamic-update-slice | bytes 1572868 | tf_op jit(solution)/shard_map/jvp()/while/body/jit(dynamic_update_index_in_dim)/dynamic_update_slice | solution.py:175
  263.2 17.9 %dynamic_update_slice.262 = f32[4,256,12,64]{1,0,3,2:T(4,128)} dynamic-update-slice(f32[4,256,12,64]{1,0,3,2:T(4,128)} %get-tuple-element.2368, f32[1,256,12,64]{1,0,3,2:T(1,128)S(1)} %copy.287, s32[]{:T(128)S(6)} %copy.359, s32[]{:T(128)} %constant.380.clone.1..sunk, s32[]{:T(128)} %constant.380.clone.1..sunk, s32[]{:T(128)} %constant.380.clone.1..sunk) | dynamic-update-slice | bytes 1572868 | tf_op jit(solution)/shard_map/jvp()/while/body/jit(dynamic_update_index_in_dim)/dynamic_update_slice | solution.py:175
  307.3 5.0 fusion.272
  313.1 17.9 %dynamic_update_slice.262 = f32[4,256,12,64]{1,0,3,2:T(4,128)} dynamic-update-slice(f32[4,256,12,64]{1,0,3,2:T(4,128)} %get-tuple-element.2368, f32[1,256,12,64]{1,0,3,2:T(1,128)S(1)} %copy.287, s32[]{:T(128)S(6)} %copy.359, s32[]{:T(128)} %constant.380.clone.1..sunk, s32[]{:T(128)} %constant.380.clone.1..sunk, s32[]{:T(128)} %constant.380.clone.1..sunk) | dynamic-update-slice | bytes 1572868 | tf_op jit(solution)/shard_map/jvp()/while/body/jit(dynamic_update_index_in_dim)/dynamic_update_slice | solution.py:175
  357.7 21.5 %collective-permute-done.19 = bf16[4,2,48,1536]{3,2,1,0:T(8,128)(2,1)S(1)} collective-permute-done((bf16[4,2,48,1536]{3,2,1,0:T(8,128)(2,1)}, bf16[4,2,48,1536]{3,2,1,0:T(8,128)(2,1)S(1)}, u32[]{:S(2)}, u32[]{:S(2)}) %collective-permute-start.19) | collective-permute-done | bytes 1179680 | tf_op jit(solution)/shard_map/ppermute | solution.py:21
  411.3 7.1 convolution_convert_fusion.1
  434.9 5.2 reshape.904
  444.1 217.6 %while.83 = (s32[]{:T(128)}, f32[12]{0:T(128)S(1)}, f32[12,128,64]{1,2,0:T(8,128)S(1)}, f32[4,256,12,64]{1,0,3,2:T(4,128)}, f32[4,256,128]{2,1,0:T(8,128)}, /*in...) while((s32[]{:T(128)}, f32[12]{0:T(128)S(1)}, ...), condition=%wide.region_19.20_spmd.clone, body=%wide.region_7.19_spmd.clone.sunk | while | flops 2628679680 | bytes 31409684 | solution.py:175
  459.8 17.9 %dynamic_update_slice.268 = f32[4,256,12,64]{1,0,3,2:T(4,128)} dynamic-update-slice(f32[4,256,12,64]{1,0,3,2:T(4,128)} %get-tuple-element.2477, f32[1,256,12,64]{1,0,3,2:T(1,128)S(1)} %copy.292, s32[]{:T(128)S(6)} %sub.252, s32[]{:T(128)} %constant.380.clone.1..sunk.1, s32[]{:T(128)} %constant.380.clone.1..sunk.1, s32[]{:T(128)} %constant.380.clone.1..sunk.1) | dynamic-update-slice | bytes 1572868 | tf_op jit(solution)/shard_map/transpose(jvp())/while/body/jit(dynamic_update_index_in_dim)/dynamic_update_slice | solution.py:175
  479.4 6.5 fusion.290
  514.0 17.9 %dynamic_update_slice.268 = f32[4,256,12,64]{1,0,3,2:T(4,128)} dynamic-update-slice(f32[4,256,12,64]{1,0,3,2:T(4,128)} %get-tuple-element.2477, f32[1,256,12,64]{1,0,3,2:T(1,128)S(1)} %copy.292, s32[]{:T(128)S(6)} %sub.252, s32[]{:T(128)} %constant.380.clone.1..sunk.1, s32[]{:T(128)} %constant.380.clone.1..sunk.1, s32[]{:T(128)} %constant.380.clone.1..sunk.1) | dynamic-update-slice | bytes 1572868 | tf_op jit(solution)/shard_map/transpose(jvp())/while/body/jit(dynamic_update_index_in_dim)/dynamic_update_slice | solution.py:175
  533.6 6.5 fusion.290
  568.3 17.9 %dynamic_update_slice.268 = f32[4,256,12,64]{1,0,3,2:T(4,128)} dynamic-update-slice(f32[4,256,12,64]{1,0,3,2:T(4,128)} %get-tuple-element.2477, f32[1,256,12,64]{1,0,3,2:T(1,128)S(1)} %copy.292, s32[]{:T(128)S(6)} %sub.252, s32[]{:T(128)} %constant.380.clone.1..sunk.1, s32[]{:T(128)} %constant.380.clone.1..sunk.1, s32[]{:T(128)} %constant.380.clone.1..sunk.1) | dynamic-update-slice | bytes 1572868 | tf_op jit(solution)/shard_map/transpose(jvp())/while/body/jit(dynamic_update_index_in_dim)/dynamic_update_slice | solution.py:175
  587.9 6.5 fusion.290
  622.5 17.9 %dynamic_update_slice.268 = f32[4,256,12,64]{1,0,3,2:T(4,128)} dynamic-update-slice(f32[4,256,12,64]{1,0,3,2:T(4,128)} %get-tuple-element.2477, f32[1,256,12,64]{1,0,3,2:T(1,128)S(1)} %copy.292, s32[]{:T(128)S(6)} %sub.252, s32[]{:T(128)} %constant.380.clone.1..sunk.1, s32[]{:T(128)} %constant.380.clone.1..sunk.1, s32[]{:T(128)} %constant.380.clone.1..sunk.1) | dynamic-update-slice | bytes 1572868 | tf_op jit(solution)/shard_map/transpose(jvp())/while/body/jit(dynamic_update_index_in_dim)/dynamic_update_slice | solution.py:175
  642.1 6.5 fusion.290
  663.8 5.2 multiply_reduce_fusion.11
  678.2 6.7 multiply_reduce_fusion.5
  695.4 9.6 %multiply_reduce_fusion = (f32[1536]{0:T(1024)}, bf16[1024,1536]{1,0:T(8,128)(2,1)}) fusion(bf16[1024,1536]{1,0:T(8,128)(2,1)S(1)} %bitcast.724, f32[1024,1536]{1,0:T(8,128)} %fusion.145, bf16[1536,1152]{1,0:T(8,128)(2,1)S(1)} %bitcast.719, bf16[1024,12]{1,0:T(8,128)(2,1)S(1)} %get-tuple-element.1756, bf16[1024,256]{1,0:T(8,128)(2,1)S(1)} %fusion.172, ...), kind=kOutput, calls=%fused_computation.193 | convolution fusion | flops 3641178624 | bytes 18249728 | tf_op jit(solution)/shard_map/dot_general | solution.py:292
  711.8 7.2 convolution_convert_fusion.3
  765.2 33.6 %collective-permute-done.40 = bf16[4,2,48,1536]{3,2,1,0:T(8,128)(2,1)} collective-permute-done((bf16[4,2,48,1536]{3,2,1,0:T(8,128)(2,1)}, bf16[4,2,48,1536]{3,2,1,0:T(8,128)(2,1)}, u32[]{:S(2)}, u32[]{:S(2)}) %collective-permute-start.40) | collective-permute-done | bytes 1179680 | tf_op jit(solution)/shard_map/ppermute | solution.py:21
  807.6 9.9 %collective-permute-done.49 = bf16[4,2,48,896]{3,2,1,0:T(8,128)(2,1)} collective-permute-done((bf16[4,2,48,896]{3,2,1,0:T(8,128)(2,1)}, bf16[4,2,48,896]{3,2,1,0:T(8,128)(2,1)}, u32[]{:S(2)}, u32[]{:S(2)}) %collective-permute-start.49) | collective-permute-done | bytes 688160 | tf_op jit(solution)/shard_map/ppermute | solution.py:21
  817.7 11.9 %collective-permute-done.47 = bf16[4,2,48,896]{3,2,1,0:T(8,128)(2,1)} collective-permute-done((bf16[4,2,48,896]{3,2,1,0:T(8,128)(2,1)S(1)}, bf16[4,2,48,896]{3,2,1,0:T(8,128)(2,1)}, u32[]{:S(2)}, u32[]{:S(2)}) %collective-permute-start.47) | collective-permute-done | bytes 688160 | tf_op jit(solution)/shard_map/ppermute | solution.py:21
  835.1 5.3 collective-permute-done.52
  844.6 8.8 collective-permute-done.43
  871.2 13.9 %collective-permute-done.28 = bf16[256,1536]{1,0:T(8,128)(2,1)S(1)} collective-permute-done((bf16[256,1536]{1,0:T(8,128)(2,1)S(1)}, bf16[256,1536]{1,0:T(8,128)(2,1)S(1)}, u32[]{:S(2)}, u32[]{:S(2)}) %collective-permute-start.28) | collective-permute-done | bytes 786464 | tf_op jit(solution)/shard_map/ppermute | solution.py:21
  885.5 9.0 %collective-permute-done.26 = bf16[256,1536]{1,0:T(8,128)(2,1)S(1)} collective-permute-done((bf16[256,1536]{1,0:T(8,128)(2,1)S(1)}, bf16[256,1536]{1,0:T(8,128)(2,1)S(1)}, u32[]{:S(2)}, u32[]{:S(2)}) %collective-permute-start.26) | collective-permute-done | bytes 786464 | tf_op jit(solution)/shard_map/ppermute | solution.py:21
  (776 shorter events, 512.2 us)
Async XLA Ops:
  13.5 26.5 %collective-permute-start.1 = (bf16[256,1536]{1,0:T(8,128)(2,1)}, bf16[256,1536]{1,0:T(8,128)(2,1)}, u32[]{:S(2)}, u32[]{:S(2)}) collective-permute-start(bf16[256,1536]{1,0:T(8,128)(2,1)} %fusion.151), channel_id=1, source_target_pairs={{0,2},{2,0},{1,3},{3,1},{4,6},{6,4},{5,7},{7,5},{8,10},{10,8},{9,1... | collective-permute-start | bytes 2359304 | tf_op jit(solution)/shard_map/ppermute | solution.py:21
  15.2 68.5 %collective-permute-start = (bf16[256,1536]{1,0:T(8,128)(2,1)}, bf16[256,1536]{1,0:T(8,128)(2,1)}, u32[]{:S(2)}, u32[]{:S(2)}) collective-permute-start(bf16[256,1536]{1,0:T(8,128)(2,1)} %fusion.151), channel_id=1, source_target_pairs={{0,1},{1,0},{2,3},{3,2},{4,5},{5,4},{6,7},{7,6},{8,9},{9,8},{10,11... | collective-permute-start | bytes 2359304 | tf_op jit(solution)/shard_map/ppermute | solution.py:21
  15.6 12.7 %collective-permute-start.7 = (bf16[2,48,1152]{2,1,0:T(8,128)(2,1)S(1)}, bf16[2,48,1152]{2,1,0:T(8,128)(2,1)S(1)}, u32[]{:S(2)}, u32[]{:S(2)}) collective-permute-start(bf16[2,48,1152]{2,1,0:T(8,128)(2,1)S(1)} %pad_maximum_fusion.9), channel_id=1, source_target_pairs={{0,24},{8,0},{16,8},{24,16},{1,25},{9,1},{17,9},{25,17},{2,26},{10... | collective-permute-start | bytes 663560 | tf_op jit(solution)/shard_map/ppermute | solution.py:21
  19.3 12.7 %collective-permute-start.9 = (bf16[2,48,1152]{2,1,0:T(8,128)(2,1)S(1)}, bf16[2,48,1152]{2,1,0:T(8,128)(2,1)S(1)}, u32[]{:S(2)}, u32[]{:S(2)}) collective-permute-start(bf16[2,48,1152]{2,1,0:T(8,128)(2,1)S(1)} %pad_maximum_fusion.9), channel_id=1, source_target_pairs={{0,8},{8,16},{16,24},{24,0},{1,9},{9,17},{17,25},{25,1},{2,10},{10... | collective-permute-start | bytes 663560 | tf_op jit(solution)/shard_map/ppermute | solution.py:21
  33.1 41.8 %collective-permute-start.10 = (bf16[4,2,48,1152]{3,2,1,0:T(8,128)(2,1)S(1)}, bf16[4,2,48,1152]{3,2,1,0:T(8,128)(2,1)S(1)}, u32[]{:S(2)}, u32[]{:S(2)}) collective-permute-start(bf16[4,2,48,1152]{3,2,1,0:T(8,128)(2,1)S(1)} %get-tuple-element.1769), channel_id=1, source_target_pairs={{0,96},{32,0},{64,32},{96,64},{1,97},{33,1},{65,33},{97,65},{2,98}... | collective-permute-start | bytes 2654216 | tf_op jit(solution)/shard_map/ppermute | solution.py:21
  35.3 40.7 %collective-permute-start.11 = (bf16[4,2,48,1152]{3,2,1,0:T(8,128)(2,1)S(1)}, bf16[4,2,48,1152]{3,2,1,0:T(8,128)(2,1)S(1)}, u32[]{:S(2)}, u32[]{:S(2)}) collective-permute-start(bf16[4,2,48,1152]{3,2,1,0:T(8,128)(2,1)S(1)} %get-tuple-element.1769), channel_id=1, source_target_pairs={{0,64},{32,96},{64,0},{96,32},{1,65},{33,97},{65,1},{97,33},{2,66}... | collective-permute-start | bytes 2654216 | tf_op jit(solution)/shard_map/ppermute | solution.py:21
  37.7 39.3 %collective-permute-start.12 = (bf16[4,2,48,1152]{3,2,1,0:T(8,128)(2,1)S(1)}, bf16[4,2,48,1152]{3,2,1,0:T(8,128)(2,1)S(1)}, u32[]{:S(2)}, u32[]{:S(2)}) collective-permute-start(bf16[4,2,48,1152]{3,2,1,0:T(8,128)(2,1)S(1)} %get-tuple-element.1769), channel_id=1, source_target_pairs={{0,32},{32,64},{64,96},{96,0},{1,33},{33,65},{65,97},{97,1},{2,34}... | collective-permute-start | bytes 2654216 | tf_op jit(solution)/shard_map/ppermute | solution.py:21
  40.0 52.7 %collective-permute-start.2 = (bf16[256,1536]{1,0:T(8,128)(2,1)}, bf16[256,1536]{1,0:T(8,128)(2,1)S(1)}, u32[]{:S(2)}, u32[]{:S(2)}) collective-permute-start(bf16[256,1536]{1,0:T(8,128)(2,1)} %collective-permute-done.1), channel_id=1, source_target_pairs={{0,1},{1,0},{2,3},{3,2},{4,5},{5,4},{6,7},{7,6},{8,9},{9,8},{10,11... | collective-permute-start | bytes 2359304 | tf_op jit(solution)/shard_map/ppermute | solution.py:21
  89.4 32.8 %collective-permute-start.14 = (bf16[2,48,1536]{2,1,0:T(8,128)(2,1)}, bf16[2,48,1536]{2,1,0:T(8,128)(2,1)}, u32[]{:S(2)}, u32[]{:S(2)}) collective-permute-start(bf16[2,48,1536]{2,1,0:T(8,128)(2,1)} %pad_maximum_fusion.7), channel_id=1, source_target_pairs={{0,24},{8,0},{16,8},{24,16},{1,25},{9,1},{17,9},{25,17},{2,26},{10... | collective-permute-start | bytes 884744 | tf_op jit(solution)/shard_map/ppermute | solution.py:21
  89.4 34.6 %collective-permute-start.15 = (bf16[2,48,1536]{2,1,0:T(8,128)(2,1)}, bf16[2,48,1536]{2,1,0:T(8,128)(2,1)}, u32[]{:S(2)}, u32[]{:S(2)}) collective-permute-start(bf16[2,48,1536]{2,1,0:T(8,128)(2,1)} %pad_maximum_fusion.7), channel_id=1, source_target_pairs={{0,16},{8,24},{16,0},{24,8},{1,17},{9,25},{17,1},{25,9},{2,18},{10... | collective-permute-start | bytes 884744 | tf_op jit(solution)/shard_map/ppermute | solution.py:21
  90.2 35.5 %collective-permute-start.16 = (bf16[2,48,1536]{2,1,0:T(8,128)(2,1)}, bf16[2,48,1536]{2,1,0:T(8,128)(2,1)}, u32[]{:S(2)}, u32[]{:S(2)}) collective-permute-start(bf16[2,48,1536]{2,1,0:T(8,128)(2,1)} %pad_maximum_fusion.7), channel_id=1, source_target_pairs={{0,8},{8,16},{16,24},{24,0},{1,9},{9,17},{17,25},{25,1},{2,10},{10... | collective-permute-start | bytes 884744 | tf_op jit(solution)/shard_map/ppermute | solution.py:21
  99.1 252.1 %collective-permute-start.21 = (bf16[256,1536]{1,0:T(8,128)(2,1)}, bf16[256,1536]{1,0:T(8,128)(2,1)}, u32[]{:S(2)}, u32[]{:S(2)}) collective-permute-start(bf16[256,1536]{1,0:T(8,128)(2,1)} %param.30), channel_id=1, source_target_pairs={{0,2},{2,0},{1,3},{3,1},{4,6},{6,4},{5,7},{7,5},{8,10},{10,8},{9,1... | collective-permute-start | bytes 2359304 | tf_op jit(solution)/shard_map/ppermute | solution.py:21
  101.0 250.5 %collective-permute-start.20 = (bf16[256,1536]{1,0:T(8,128)(2,1)}, bf16[256,1536]{1,0:T(8,128)(2,1)}, u32[]{:S(2)}, u32[]{:S(2)}) collective-permute-start(bf16[256,1536]{1,0:T(8,128)(2,1)} %param.30), channel_id=1, source_target_pairs={{0,1},{1,0},{2,3},{3,2},{4,5},{5,4},{6,7},{7,6},{8,9},{9,8},{10,11... | collective-permute-start | bytes 2359304 | tf_op jit(solution)/shard_map/ppermute | solution.py:21
  134.5 218.4 %collective-permute-start.17 = (bf16[4,2,48,1536]{3,2,1,0:T(8,128)(2,1)}, bf16[4,2,48,1536]{3,2,1,0:T(8,128)(2,1)}, u32[]{:S(2)}, u32[]{:S(2)}) collective-permute-start(bf16[4,2,48,1536]{3,2,1,0:T(8,128)(2,1)} %get-tuple-element.1767), channel_id=1, source_target_pairs={{0,96},{32,0},{64,32},{96,64},{1,97},{33,1},{65,33},{97,65},{2,98}... | collective-permute-start | bytes 3538952 | tf_op jit(solution)/shard_map/ppermute | solution.py:21
  135.7 219.6 %collective-permute-start.18 = (bf16[4,2,48,1536]{3,2,1,0:T(8,128)(2,1)}, bf16[4,2,48,1536]{3,2,1,0:T(8,128)(2,1)}, u32[]{:S(2)}, u32[]{:S(2)}) collective-permute-start(bf16[4,2,48,1536]{3,2,1,0:T(8,128)(2,1)} %get-tuple-element.1767), channel_id=1, source_target_pairs={{0,64},{32,96},{64,0},{96,32},{1,65},{33,97},{65,1},{97,33},{2,66}... | collective-permute-start | bytes 3538952 | tf_op jit(solution)/shard_map/ppermute | solution.py:21
  351.2 28.0 %collective-permute-start.19 = (bf16[4,2,48,1536]{3,2,1,0:T(8,128)(2,1)}, bf16[4,2,48,1536]{3,2,1,0:T(8,128)(2,1)S(1)}, u32[]{:S(2)}, u32[]{:S(2)}) collective-permute-start(bf16[4,2,48,1536]{3,2,1,0:T(8,128)(2,1)} %get-tuple-element.1767), channel_id=1, source_target_pairs={{0,32},{32,64},{64,96},{96,0},{1,33},{33,65},{65,97},{97,1},{2,34}... | collective-permute-start | bytes 3538952 | tf_op jit(solution)/shard_map/ppermute | solution.py:21
  351.2 42.2 %collective-permute-start.22 = (bf16[256,1536]{1,0:T(8,128)(2,1)}, bf16[256,1536]{1,0:T(8,128)(2,1)S(1)}, u32[]{:S(2)}, u32[]{:S(2)}) collective-permute-start(bf16[256,1536]{1,0:T(8,128)(2,1)} %collective-permute-done.21), channel_id=1, source_target_pairs={{0,1},{1,0},{2,3},{3,2},{4,5},{5,4},{6,7},{7,6},{8,9},{9,8},{10,11... | collective-permute-start | bytes 2359304 | tf_op jit(solution)/shard_map/ppermute | solution.py:21
  707.7 12.0 %collective-permute-start.29 = (f32[2816]{0:T(1024)}, f32[2816]{0:T(1024)}, u32[]{:S(2)}, u32[]{:S(2)}) collective-permute-start(f32[2816]{0:T(1024)} %pad_maximum_fusion.14), channel_id=1, source_target_pairs={{0,1},{1,0},{2,3},{3,2},{4,5},{5,4},{6,7},{7,6},{8,9},{9,8},{10,11... | collective-permute-start | bytes 33800 | tf_op jit(solution)/shard_map/ppermute | solution.py:21
  711.1 40.9 %collective-permute-start.45 = (bf16[2,32,12,256]{3,1,2,0:T(8,128)(2,1)}, bf16[2,32,12,256]{3,1,2,0:T(8,128)(2,1)S(1)}, u32[]{:S(2)}, u32[]{:S(2)}) collective-permute-start(bf16[2,32,12,256]{3,1,2,0:T(8,128)(2,1)} %dynamic-slice_bitcast_fusion.13), channel_id=1, source_target_pairs={{0,1},{1,0},{2,3},{3,2},{4,5},{5,4},{6,7},{7,6},{8,9},{9,8},{10,11... | collective-permute-start | bytes 1179656 | tf_op jit(solution)/shard_map/ppermute | solution.py:21
  748.2 50.6 %collective-permute-start.40 = (bf16[4,2,48,1536]{3,2,1,0:T(8,128)(2,1)}, bf16[4,2,48,1536]{3,2,1,0:T(8,128)(2,1)}, u32[]{:S(2)}, u32[]{:S(2)}) collective-permute-start(bf16[4,2,48,1536]{3,2,1,0:T(8,128)(2,1)} %get-tuple-element.1798), channel_id=1, source_target_pairs={{0,32},{32,64},{64,96},{96,0},{1,33},{33,65},{65,97},{97,1},{2,34}... | collective-permute-start | bytes 3538952 | tf_op jit(solution)/shard_map/ppermute | solution.py:21
  748.5 55.7 %collective-permute-start.39 = (bf16[4,2,48,1536]{3,2,1,0:T(8,128)(2,1)}, bf16[4,2,48,1536]{3,2,1,0:T(8,128)(2,1)}, u32[]{:S(2)}, u32[]{:S(2)}) collective-permute-start(bf16[4,2,48,1536]{3,2,1,0:T(8,128)(2,1)} %get-tuple-element.1797), channel_id=1, source_target_pairs={{0,96},{32,0},{64,32},{96,64},{1,97},{33,1},{65,33},{97,65},{2,98}... | collective-permute-start | bytes 3538952 | tf_op jit(solution)/shard_map/ppermute | solution.py:21
  750.2 54.0 %collective-permute-start.38 = (bf16[4,2,48,1536]{3,2,1,0:T(8,128)(2,1)}, bf16[4,2,48,1536]{3,2,1,0:T(8,128)(2,1)}, u32[]{:S(2)}, u32[]{:S(2)}) collective-permute-start(bf16[4,2,48,1536]{3,2,1,0:T(8,128)(2,1)} %get-tuple-element.1796), channel_id=1, source_target_pairs={{0,64},{32,96},{64,0},{96,32},{1,65},{33,97},{65,1},{97,33},{2,66}... | collective-permute-start | bytes 3538952 | tf_op jit(solution)/shard_map/ppermute | solution.py:21
  763.2 54.3 %collective-permute-start.49 = (bf16[4,2,48,896]{3,2,1,0:T(8,128)(2,1)}, bf16[4,2,48,896]{3,2,1,0:T(8,128)(2,1)}, u32[]{:S(2)}, u32[]{:S(2)}) collective-permute-start(bf16[4,2,48,896]{3,2,1,0:T(8,128)(2,1)} %get-tuple-element.1808), channel_id=1, source_target_pairs={{0,32},{32,64},{64,96},{96,0},{1,33},{33,65},{65,97},{97,1},{2,34}... | collective-permute-start | bytes 2064392 | tf_op jit(solution)/shard_map/ppermute | solution.py:21
  764.5 53.1 %collective-permute-start.48 = (bf16[4,2,48,896]{3,2,1,0:T(8,128)(2,1)}, bf16[4,2,48,896]{3,2,1,0:T(8,128)(2,1)}, u32[]{:S(2)}, u32[]{:S(2)}) collective-permute-start(bf16[4,2,48,896]{3,2,1,0:T(8,128)(2,1)} %get-tuple-element.1809), channel_id=1, source_target_pairs={{0,96},{32,0},{64,32},{96,64},{1,97},{33,1},{65,33},{97,65},{2,98}... | collective-permute-start | bytes 2064392 | tf_op jit(solution)/shard_map/ppermute | solution.py:21
  798.8 30.8 %collective-permute-start.47 = (bf16[4,2,48,896]{3,2,1,0:T(8,128)(2,1)S(1)}, bf16[4,2,48,896]{3,2,1,0:T(8,128)(2,1)}, u32[]{:S(2)}, u32[]{:S(2)}) collective-permute-start(bf16[4,2,48,896]{3,2,1,0:T(8,128)(2,1)S(1)} %get-tuple-element.1807), channel_id=1, source_target_pairs={{0,64},{32,96},{64,0},{96,32},{1,65},{33,97},{65,1},{97,33},{2,66}... | collective-permute-start | bytes 2064392 | tf_op jit(solution)/shard_map/ppermute | solution.py:21
  804.2 56.8 %collective-permute-start.27 = (bf16[2,256,1536]{2,1,0:T(8,128)(2,1)}, bf16[2,256,1536]{2,1,0:T(8,128)(2,1)}, u32[]{:S(2)}, u32[]{:S(2)}) collective-permute-start(bf16[2,256,1536]{2,1,0:T(8,128)(2,1)} %dynamic-slice_bitcast_fusion.6), channel_id=1, source_target_pairs={{0,1},{1,0},{2,3},{3,2},{4,5},{5,4},{6,7},{7,6},{8,9},{9,8},{10,11... | collective-permute-start | bytes 4718600 | tf_op jit(solution)/shard_map/ppermute | solution.py:21
  804.2 60.5 %collective-permute-start.25 = (bf16[2,256,1536]{2,1,0:T(8,128)(2,1)}, bf16[2,256,1536]{2,1,0:T(8,128)(2,1)}, u32[]{:S(2)}, u32[]{:S(2)}) collective-permute-start(bf16[2,256,1536]{2,1,0:T(8,128)(2,1)} %dynamic-slice_bitcast_fusion.7), channel_id=1, source_target_pairs={{0,1},{1,0},{2,3},{3,2},{4,5},{5,4},{6,7},{7,6},{8,9},{9,8},{10,11... | collective-permute-start | bytes 4718600 | tf_op jit(solution)/shard_map/ppermute | solution.py:21
  840.3 13.1 %collective-permute-start.43 = (bf16[2,48,1536]{2,1,0:T(8,128)(2,1)S(1)}, bf16[2,48,1536]{2,1,0:T(8,128)(2,1)S(1)}, u32[]{:S(2)}, u32[]{:S(2)}) collective-permute-start(bf16[2,48,1536]{2,1,0:T(8,128)(2,1)S(1)} %get-tuple-element.1819), channel_id=1, source_target_pairs={{0,8},{8,16},{16,24},{24,0},{1,9},{9,17},{17,25},{25,1},{2,10},{10... | collective-permute-start | bytes 884744 | tf_op jit(solution)/shard_map/ppermute | solution.py:21
  840.4 13.3 %collective-permute-start.42 = (bf16[2,48,1536]{2,1,0:T(8,128)(2,1)S(1)}, bf16[2,48,1536]{2,1,0:T(8,128)(2,1)S(1)}, u32[]{:S(2)}, u32[]{:S(2)}) collective-permute-start(bf16[2,48,1536]{2,1,0:T(8,128)(2,1)S(1)} %get-tuple-element.1820), channel_id=1, source_target_pairs={{0,24},{8,0},{16,8},{24,16},{1,25},{9,1},{17,9},{25,17},{2,26},{10... | collective-permute-start | bytes 884744 | tf_op jit(solution)/shard_map/ppermute | solution.py:21
  854.5 14.1 %collective-permute-start.44 = (bf16[48,1536]{1,0:T(8,128)(2,1)}, bf16[48,1536]{1,0:T(8,128)(2,1)}, u32[]{:S(2)}, u32[]{:S(2)}) collective-permute-start(bf16[48,1536]{1,0:T(8,128)(2,1)} %dynamic-slice_bitcast_fusion.21), channel_id=1, source_target_pairs={{0,4},{4,0},{1,5},{5,1},{2,6},{6,2},{3,7},{7,3},{8,12},{12,8},{9,1... | collective-permute-start | bytes 442376 | tf_op jit(solution)/shard_map/ppermute | solution.py:21
  863.0 22.1 %collective-permute-start.28 = (bf16[256,1536]{1,0:T(8,128)(2,1)S(1)}, bf16[256,1536]{1,0:T(8,128)(2,1)S(1)}, u32[]{:S(2)}, u32[]{:S(2)}) collective-permute-start(bf16[256,1536]{1,0:T(8,128)(2,1)S(1)} %dynamic-slice_bitcast_fusion.8), channel_id=1, source_target_pairs={{0,2},{2,0},{1,3},{3,1},{4,6},{6,4},{5,7},{7,5},{8,10},{10,8},{9,1... | collective-permute-start | bytes 2359304 | tf_op jit(solution)/shard_map/ppermute | solution.py:21
  866.7 27.9 %collective-permute-start.26 = (bf16[256,1536]{1,0:T(8,128)(2,1)S(1)}, bf16[256,1536]{1,0:T(8,128)(2,1)S(1)}, u32[]{:S(2)}, u32[]{:S(2)}) collective-permute-start(bf16[256,1536]{1,0:T(8,128)(2,1)S(1)} %dynamic-slice_bitcast_fusion.9), channel_id=1, source_target_pairs={{0,2},{2,0},{1,3},{3,1},{4,6},{6,4},{5,7},{7,5},{8,10},{10,8},{9,1... | collective-permute-start | bytes 2359304 | tf_op jit(solution)/shard_map/ppermute | solution.py:21
  (124 other events, 2063.4 us)

commit v2 on v1

v2 whole, which is shorter than its diff:
```python
import jax
import jax.numpy as jnp
from jax import lax
from jax.experimental import pallas as pl
from jax.experimental.pallas import tpu as pltpu
from jax.sharding import Mesh
from jax.sharding import PartitionSpec as P

EPS = 1e-05
DP = ("y", "x", "zl")
TENSOR = ("zh", "c")
SIZES = {"y": 4, "x": 4, "zl": 2, "zh": 2, "c": 2}

F32 = jnp.float32
BF16 = jnp.bfloat16
HIGH = lax.Precision.HIGHEST
BLOCK = 128
VMEM = 56 * 1024 * 1024
NT = (((1,), (1,)), ((), ()))


def dot(a, b):
    return jnp.dot(a, b, preferred_element_type=F32)


def dot_nt(a, b):
    return lax.dot_general(a, b, NT, preferred_element_type=F32)


def sigmoid(a):
    return 0.5 * jnp.tanh(0.5 * a) + 0.5


def softplus(a):
    return jnp.maximum(a, 0.0) + jnp.log1p(jnp.exp(-jnp.abs(a)))


def conv_strip(ext, taps, aux, j):
    n = ext.shape[0] - 8
    lanes = slice(j * 128, (j + 1) * 128)
    total = taps[4:5, lanes] + taps[3:4, lanes] * ext[8 : 8 + n, lanes]
    for back in (1, 2, 3):
        total += taps[3 - back : 4 - back, lanes] * (
            aux[:, back - 1 : back] * ext[8 - back : 8 - back + n, lanes]
        )
    return total


def spread_heads(cols, j, low_half):
    return jnp.where(low_half, cols[:, 2 * j : 2 * j + 1], cols[:, 2 * j + 1 : 2 * j + 2])


def scan_forward_kernel(tok, weights_a, weights_b, taps, heads, chan, aux, segrow, pre_out, scan_out, state_out, ext, act, carry, fed):
    n = tok.shape[0]
    pairs = carry.shape[1] // 128

    @pl.when(pl.program_id(0) == 0)
    def _():
        carry[...] = jnp.zeros_like(carry)
        ext[0:8, :] = jnp.zeros((8, ext.shape[1]), F32)

    pre = jnp.concatenate([dot(tok[...], weights_a[...]), dot(tok[...], weights_b[...])], 1)
    pre_out[...] = pre
    wide = ext.shape[1]
    ext[8:, :] = pre[:, :wide]
    marks = aux[...]
    for j in range(wide // 128):
        total = conv_strip(ext, taps, marks, j)
        act[:, j * 128 : (j + 1) * 128] = total * sigmoid(total)
    ext[0:8, :] = ext[n : n + 8, :]

    step = softplus(pre[:, wide:] + heads[0:1, :])
    log_step = -step * heads[1:2, :]
    row = lax.broadcasted_iota(jnp.int32, (n, n), 0)
    col = lax.broadcasted_iota(jnp.int32, (n, n), 1)
    lower = (row >= col).astype(F32)
    cum = jnp.dot(lower, log_step, precision=HIGH, preferred_element_type=F32)
    cum_t = cum.T
    write = act[:, pairs * 128 : (pairs + 1) * 128]
    read = act[:, (pairs + 1) * 128 : (pairs + 2) * 128].astype(BF16)
    write_t = write.T.astype(BF16)
    allowed = (row >= col) & (marks[:, 8:9] == segrow[0:1, :])
    inner = jnp.where(allowed, dot(read, write_t), 0.0)
    last = cum[n - 1 : n, :]
    enters = jnp.exp(cum) * marks[:, 3:4]
    to_end = jnp.exp(last - cum) * marks[:, 4:5]
    keep = jnp.exp(last) * marks[n - 1 : n, 3:4]
    held = carry[...]
    held_low = held.astype(BF16)
    state_out[0] = held_low
    from_state = dot(read, held_low)
    low_half = lax.broadcasted_iota(jnp.int32, (1, 128), 1) < 64
    for j in range(pairs):
        lanes = slice(j * 128, (j + 1) * 128)
        x = act[:, lanes]
        xdt = x * spread_heads(step, j, low_half)
        parts = []
        for h in (2 * j, 2 * j + 1):
            decay = jnp.exp(jnp.minimum(cum[:, h : h + 1] - cum_t[h : h + 1, :], 0.0))
            parts.append((decay * inner).astype(BF16))
        xdt_low = xdt.astype(BF16)
        zero = jnp.zeros_like(xdt_low)
        pair = jnp.concatenate([jnp.where(low_half, xdt_low, zero), jnp.where(low_half, zero, xdt_low)], 0)
        y = dot(jnp.concatenate(parts, 1), pair)
        y += spread_heads(enters, j, low_half) * from_state[:, lanes] + chan[0:1, lanes] * x
        scan_out[:, lanes] = y
        fed[:, lanes] = (xdt * spread_heads(to_end, j, low_half)).astype(BF16)
        carry[:, lanes] = held[:, lanes] * spread_heads(keep, j, low_half)
    carry[...] += dot(write_t, fed[...])


def scan_backward_kernel(pre, pre_before, taps, heads, chan, sums, aux, segrow, grad, state, low_out, taps_out, heads_out, ext, gext, act, slope, carry, fed, back, rows):
    n = pre.shape[0]
    pairs = carry.shape[1] // 128
    wide = ext.shape[1]

    @pl.when(pl.program_id(0) == 0)
    def _():
        carry[...] = jnp.zeros_like(carry)
        gext[n:, :] = jnp.zeros((8, wide), F32)
        taps_out[...] = jnp.zeros_like(taps_out)
        heads_out[...] = jnp.zeros_like(heads_out)
        rows[...] = jnp.zeros_like(rows)

    marks = aux[...]
    ext[0:8, :] = pre_before[:, :wide]
    ext[8:, :] = pre[:, :wide]
    for j in range(wide // 128):
        lanes = slice(j * 128, (j + 1) * 128)
        total = conv_strip(ext, taps, marks, j)
        sig = sigmoid(total)
        value = total * sig
        act[:, lanes] = value
        slope[:, lanes] = sig + value * (1.0 - sig)

    step_arg = pre[:, wide:] + heads[0:1, :]
    step = softplus(step_arg)
    rate = heads[1:2, :]
    row = lax.broadcasted_iota(jnp.int32, (n, n), 0)
    col = lax.broadcasted_iota(jnp.int32, (n, n), 1)
    lower = (row >= col).astype(F32)
    cum = jnp.dot(lower, -step * rate, precision=HIGH, preferred_element_type=F32)
    cum_t = cum.T
    write = act[:, pairs * 128 : (pairs + 1) * 128]
    read = act[:, (pairs + 1) * 128 : (pairs + 2) * 128]
    read_t = read.T.astype(BF16)
    write_low = write.astype(BF16)
    read_low = read.astype(BF16)
    allowed = (row <= col) & (marks[:, 8:9] == segrow[0:1, :])
    inner_t = jnp.where(allowed, dot(write_low, read_t), 0.0)
    last = cum[n - 1 : n, :]
    enters = jnp.exp(cum) * marks[:, 3:4]
    to_end = jnp.exp(last - cum) * marks[:, 4:5]
    keep = jnp.exp(last) * marks[n - 1 : n, 3:4]
    held = state[0]
    later = carry[...]
    later_low = later.astype(BF16)
    from_state = dot(read_low, held)
    from_later = dot(write_low, later_low)
    low_half = lax.broadcasted_iota(jnp.int32, (1, 128), 1) < 64
    head_lane = lax.broadcasted_iota(jnp.int32, (1, 128), 1)
    grad_inner = jnp.zeros((n, n), F32)
    col_sums = jnp.zeros((n, 128), F32)
    to_end_part = jnp.zeros((n, 128), F32)
    enter_part = jnp.zeros((n, 128), F32)
    step_part = jnp.zeros((n, 128), F32)
    skip_part = jnp.zeros((n, 128), F32)
    keep_part = jnp.zeros((8, 128), F32)

    def head_sums(value, j):
        high = value.astype(BF16)
        rest = (value - high.astype(F32)).astype(BF16)
        return dot(jnp.concatenate([high, rest], 1), sums[j])

    for j in range(pairs):
        lanes = slice(j * 128, (j + 1) * 128)
        x = act[:, lanes]
        dy = grad[:, lanes].astype(F32)
        step_wide = spread_heads(step, j, low_half)
        xdt = x * step_wide
        xdt_low = xdt.astype(BF16)
        dy_low = dy.astype(BF16)
        zero = jnp.zeros_like(xdt_low)
        products = dot_nt(
            jnp.concatenate([jnp.where(low_half, xdt_low, zero), jnp.where(low_half, zero, xdt_low)], 0),
            dy_low,
        )
        parts = []
        for k, h in enumerate((2 * j, 2 * j + 1)):
            product = products[k * n : (k + 1) * n, :]
            decay = jnp.exp(jnp.minimum(cum_t[h : h + 1, :] - cum[:, h : h + 1], 0.0))
            scaled = decay * product
            grad_inner += scaled
            weighted = scaled * inner_t
            rows[h : h + 1, :] = jnp.sum(weighted, axis=0, keepdims=True)
            col_sums += jnp.where(head_lane == h, jnp.sum(weighted, axis=1, keepdims=True), 0.0)
            parts.append((decay * inner_t).astype(BF16))
        grad_pair = jnp.concatenate([jnp.where(low_half, dy_low, zero), jnp.where(low_half, zero, dy_low)], 0)
        grad_xdt = dot(jnp.concatenate(parts, 1), grad_pair)
        end_wide = spread_heads(to_end, j, low_half)
        enter_wide = spread_heads(enters, j, low_half)
        later_part = end_wide * from_later[:, lanes]
        grad_xdt += later_part
        to_end_part += head_sums(later_part * xdt, j)
        fed[:, lanes] = (xdt * end_wide).astype(BF16)
        grad_enter = dy * enter_wide
        back[:, lanes] = grad_enter.astype(BF16)
        enter_part += head_sums(grad_enter * from_state[:, lanes], j)
        step_part += head_sums(grad_xdt * x, j)
        skip_part += head_sums(dy * x, j)
        kept = jnp.sum(held[:, lanes].astype(F32) * later[:, lanes], axis=0, keepdims=True)
        keep_part += head_sums(jnp.broadcast_to(kept, (8, 128)), j)
        act[:, lanes] = grad_xdt * step_wide + chan[0:1, lanes] * dy
        carry[:, lanes] = later[:, lanes] * spread_heads(keep, j, low_half)

    grad_cum = rows[...].T - col_sums + enter_part - to_end_part
    grad_last = jnp.sum(to_end_part, axis=0, keepdims=True) + keep * keep_part[0:1, :]
    upper = (row <= col).astype(F32)
    grad_log = jnp.dot(upper, grad_cum, precision=HIGH, preferred_element_type=F32) + grad_last
    grad_step = (step_part - rate * grad_log) * sigmoid(step_arg)
    heads_out[0:1, :] += jnp.sum(grad_step, axis=0, keepdims=True)
    heads_out[1:2, :] += -rate * jnp.sum(step * grad_log, axis=0, keepdims=True)
    heads_out[2:3, :] += jnp.sum(skip_part, axis=0, keepdims=True)
    low_out[:, wide:] = grad_step.astype(BF16)

    grad_inner = jnp.where(allowed, grad_inner, 0.0)
    act[:, pairs * 128 : (pairs + 1) * 128] = dot(grad_inner.astype(BF16), read_low) + dot_nt(fed[...], later_low)
    act[:, (pairs + 1) * 128 : (pairs + 2) * 128] = dot(grad_inner.T.astype(BF16), write_low) + dot_nt(back[...], held)
    carry[...] += dot(read_t, back[...])

    for j in range(wide // 128):
        lanes = slice(j * 128, (j + 1) * 128)
        grad_pre = act[:, lanes] * slope[:, lanes]
        gext[0:n, lanes] = grad_pre
        total = taps[3:4, lanes] * grad_pre
        taps_out[3:4, lanes] += jnp.sum(grad_pre * ext[8 : 8 + n, lanes], axis=0, keepdims=True)
        taps_out[4:5, lanes] += jnp.sum(grad_pre, axis=0, keepdims=True)
        for by in (1, 2, 3):
            total += taps[3 - by : 4 - by, lanes] * (marks[:, 4 + by : 5 + by] * gext[by : by + n, lanes])
            taps_out[3 - by : 4 - by, lanes] += jnp.sum(
                grad_pre * (marks[:, by - 1 : by] * ext[8 - by : 8 - by + n, lanes]), axis=0, keepdims=True
            )
        low_out[:, lanes] = total.astype(BF16)
    gext[n:, :] = gext[0:8, :]


def scan_marks(segments):
    length = segments.shape[0]
    blocks = segments.reshape(-1, BLOCK)
    before = jnp.concatenate([jnp.full((1,), -1, jnp.int32), blocks[:-1, -1]], 0)

    def same(by):
        if by > 0:
            other = jnp.concatenate([jnp.full((by,), -1, jnp.int32), segments[:-by]], 0)
        else:
            other = jnp.concatenate([segments[-by:], jnp.full((-by,), -1, jnp.int32)], 0)
        return other == segments

    cols = [same(1), same(2), same(3), (blocks == before[:, None]).reshape(-1), (blocks == blocks[:, -1:]).reshape(-1)]
    cols += [same(-1), same(-2), same(-3), segments]
    marks = jnp.stack([c.astype(F32) for c in cols], 1)
    return jnp.pad(marks, ((0, 0), (0, 128 - len(cols)))), jnp.broadcast_to(segments.astype(F32), (8, length))


def scan_forward(tokens, weights_a, weights_b, taps, heads, chan, marks, segrow):
    length, model = tokens.shape
    cols = weights_a.shape[1] + weights_b.shape[1]
    inner = cols - 384
    wide = cols - 128
    n = BLOCK
    blocks = length // n

    def whole(shape):
        return pl.BlockSpec(shape, lambda i: (0,) * len(shape))

    return pl.pallas_call(
        scan_forward_kernel,
        grid=(blocks,),
        in_specs=[
            pl.BlockSpec((n, model), lambda i: (i, 0)),
            whole(weights_a.shape),
            whole(weights_b.shape),
            whole((8, wide)),
            whole((8, 128)),
            whole((8, inner)),
            pl.BlockSpec((n, 128), lambda i: (i, 0)),
            pl.BlockSpec((8, n), lambda i: (0, i)),
        ],
        out_specs=[
            pl.BlockSpec((n, cols), lambda i: (i, 0)),
            pl.BlockSpec((n, inner), lambda i: (i, 0)),
            pl.BlockSpec((1, 128, inner), lambda i: (i, 0, 0)),
        ],
        out_shape=[
            jax.ShapeDtypeStruct((length, cols), F32),
            jax.ShapeDtypeStruct((length, inner), F32),
            jax.ShapeDtypeStruct((blocks, 128, inner), BF16),
        ],
        scratch_shapes=[
            pltpu.VMEM((n + 8, wide), F32),
            pltpu.VMEM((n, wide), F32),
            pltpu.VMEM((128, inner), F32),
            pltpu.VMEM((n, inner), BF16),
        ],
        compiler_params=pltpu.CompilerParams(vmem_limit_bytes=VMEM),
        name="scan_forward",
    )(tokens, weights_a, weights_b, taps, heads, chan, marks, segrow)


def scan_backward(pre, taps, heads, chan, sums, marks, segrow, grad, states):
    length, cols = pre.shape
    inner = cols - 384
    wide = cols - 128
    n = BLOCK
    blocks = length // n

    def whole(shape):
        return pl.BlockSpec(shape, lambda i: (0,) * len(shape))

    def rev(i):
        return blocks - 1 - i

    return pl.pallas_call(
        scan_backward_kernel,
        grid=(blocks,),
        in_specs=[
            pl.BlockSpec((n, cols), lambda i: (rev(i), 0)),
            pl.BlockSpec((8, cols), lambda i: (jnp.maximum(rev(i) * (n // 8) - 1, 0), 0)),
            whole((8, wide)),
            whole((8, 128)),
            whole((8, inner)),
            whole((inner // 128, 256, 128)),
            pl.BlockSpec((n, 128), lambda i: (rev(i), 0)),
            pl.BlockSpec((8, n), lambda i: (0, rev(i))),
            pl.BlockSpec((n, inner), lambda i: (rev(i), 0)),
            pl.BlockSpec((1, 128, inner), lambda i: (rev(i), 0, 0)),
        ],
        out_specs=[
            pl.BlockSpec((n, cols), lambda i: (rev(i), 0)),
            whole((8, wide)),
            whole((8, 128)),
        ],
        out_shape=[
            jax.ShapeDtypeStruct((length, cols), BF16),
            jax.ShapeDtypeStruct((8, wide), F32),
            jax.ShapeDtypeStruct((8, 128), F32),
        ],
        scratch_shapes=[
            pltpu.VMEM((n + 8, wide), F32),
            pltpu.VMEM((n + 8, wide), F32),
            pltpu.VMEM((n, wide), F32),
            pltpu.VMEM((n, wide), F32),
            pltpu.VMEM((128, inner), F32),
            pltpu.VMEM((n, inner), BF16),
            pltpu.VMEM((n, inner), BF16),
            pltpu.VMEM((128, n), F32),
        ],
        compiler_params=pltpu.CompilerParams(vmem_limit_bytes=VMEM),
        name="scan_backward",
    )(pre, pre, taps, heads, chan, sums, marks, segrow, grad, states)


def head_sum_table(inner):
    pairs = inner // 128
    lane = jnp.arange(256) % 128
    head = 2 * jnp.arange(pairs)[:, None] + (lane >= 64)[None, :]
    return (head[:, :, None] == jnp.arange(128)[None, None, :]).astype(BF16)


def mix_first_kernel(tok, rows, gate_w, out_w, scanned, gain, gate_out, mixed_out, sums_out):
    gate_pre = dot(tok[...], gate_w[...])
    grad_mixed = dot(rows[...], out_w[...])
    gate_out[...] = gate_pre
    mixed_out[...] = grad_mixed
    gated = scanned[...] * (gate_pre * sigmoid(gate_pre))
    square = jnp.sum(gated * gated, axis=1, keepdims=True)
    inner = jnp.sum(grad_mixed * gain[0:1, :] * gated, axis=1, keepdims=True)
    lane = lax.broadcasted_iota(jnp.int32, (1, 128), 1)
    cols = jnp.where(lane == 0, square, jnp.where(lane == 1, inner, 0.0))
    sums_out[...] = cols.T[0:8, :]


def mix_first(tokens, grad_rows, gate_w, out_w, scanned, gain):
    length, model = tokens.shape
    width = scanned.shape[1]
    n = 256

    def whole(shape):
        return pl.BlockSpec(shape, lambda i: (0,) * len(shape))

    def rows(cols):
        return pl.BlockSpec((n, cols), lambda i: (i, 0))

    return pl.pallas_call(
        mix_first_kernel,
        grid=(length // n,),
        in_specs=[rows(model), rows(model), whole(gate_w.shape), whole(out_w.shape), rows(width), whole((8, width))],
        out_specs=[rows(width), rows(width), pl.BlockSpec((8, n), lambda i: (0, i))],
        out_shape=[
            jax.ShapeDtypeStruct((length, width), F32),
            jax.ShapeDtypeStruct((length, width), F32),
            jax.ShapeDtypeStruct((8, length), F32),
        ],
        compiler_params=pltpu.CompilerParams(vmem_limit_bytes=VMEM),
        name="mix_first",
    )(tokens, grad_rows, gate_w, out_w, scanned, gain)


def mix_second_kernel(channels, sums, gate, grad_mixed_in, scanned_in, out_w, gain, low_out, projected, grad_scan, grad_gate, gain_out):
    n = gate.shape[0]

    @pl.when(pl.program_id(0) == 0)
    def _():
        gain_out[...] = jnp.zeros_like(gain_out)

    cols = jnp.concatenate([sums[...], jnp.zeros((120, n), F32)], 0).T
    scale = lax.rsqrt(cols[:, 0:1] / channels + EPS)
    pull = scale * scale * scale * (cols[:, 1:2] / channels)
    gate_pre = gate[...]
    grad_mixed = grad_mixed_in[...]
    scanned = scanned_in[...]
    sig = sigmoid(gate_pre)
    silu = gate_pre * sig
    gated = scanned * silu
    scaled = gated * scale
    mixed = (scaled * gain[0:1, :]).astype(BF16)
    low_out[...] = mixed
    gain_out[0:1, :] += jnp.sum(grad_mixed * scaled, axis=0, keepdims=True)
    grad_gated = scale * gain[0:1, :] * grad_mixed - gated * pull
    grad_scan[...] = grad_gated * silu
    grad_gate[...] = (grad_gated * scanned * (sig + silu * (1.0 - sig))).astype(BF16)
    projected[...] = dot_nt(mixed, out_w[...]).astype(BF16)


def mix_second(sums, gate, grad_mixed, scanned, out_w, gain, channels):
    length, width = gate.shape
    model = out_w.shape[0]
    n = 256

    def whole(shape):
        return pl.BlockSpec(shape, lambda i: (0,) * len(shape))

    def rows(cols):
        return pl.BlockSpec((n, cols), lambda i: (i, 0))

    return pl.pallas_call(
        lambda *refs: mix_second_kernel(channels, *refs),
        grid=(length // n,),
        in_specs=[pl.BlockSpec((8, n), lambda i: (0, i)), rows(width), rows(width), rows(width), whole(out_w.shape), whole((8, width))],
        out_specs=[rows(width), rows(model), rows(width), rows(width), whole((8, width))],
        out_shape=[
            jax.ShapeDtypeStruct((length, width), BF16),
            jax.ShapeDtypeStruct((length, model), BF16),
            jax.ShapeDtypeStruct((length, width), F32),
            jax.ShapeDtypeStruct((length, width), BF16),
            jax.ShapeDtypeStruct((8, width), F32),
        ],
        compiler_params=pltpu.CompilerParams(vmem_limit_bytes=VMEM),
        name="mix_second",
    )(sums, gate, grad_mixed, scanned, out_w, gain)


def token_grads_kernel(tok, grad_gate, low, gate_w, weights_a, weights_b, rows_out, sums_out):
    @pl.when(pl.program_id(0) == 0)
    def _():
        sums_out[...] = jnp.zeros_like(sums_out)

    cut = weights_a.shape[1]
    total = dot_nt(grad_gate[...], gate_w[...])
    total += dot_nt(low[:, :cut], weights_a[...])
    total += dot_nt(low[:, cut:], weights_b[...])
    rows_out[...] = total.astype(BF16)
    sums_out[0:1, :] += jnp.sum(total * tok[...].astype(F32), axis=0, keepdims=True)


def token_grads(tokens, grad_gate, low, gate_w, weights_a, weights_b):
    length, model = tokens.shape
    n = 256

    def whole(shape):
        return pl.BlockSpec(shape, lambda i: (0,) * len(shape))

    def rows(cols):
        return pl.BlockSpec((n, cols), lambda i: (i, 0))

    return pl.pallas_call(
        token_grads_kernel,
        grid=(length // n,),
        in_specs=[rows(model), rows(grad_gate.shape[1]), rows(low.shape[1]), whole(gate_w.shape), whole(weights_a.shape), whole(weights_b.shape)],
        out_specs=[rows(model), whole((8, model))],
        out_shape=[jax.ShapeDtypeStruct((length, model), BF16), jax.ShapeDtypeStruct((8, model), F32)],
        compiler_params=pltpu.CompilerParams(vmem_limit_bytes=VMEM),
        name="token_grads",
    )(tokens, grad_gate, low, gate_w, weights_a, weights_b)


def shift(value, axis, by):
    n = SIZES[axis]
    return lax.ppermute(value, axis, [(i, (i - by) % n) for i in range(n)])


def swap(value, axis):
    return shift(value, axis, 1)


def ordered_pair(own, other, axis):
    first = lax.axis_index(axis) == 0
    return jnp.stack([jnp.where(first, own, other), jnp.where(first, other, own)], 0)


def gather_pair(value, axis):
    return ordered_pair(value, swap(value, axis), axis)


def place_kernel(me, *refs):
    for k, part in enumerate(refs[:4]):

        @pl.when(pl.program_id(0) == k)
        def _():
            refs[4][...] = part[...].reshape(refs[4].shape)


def gather_ring(value, axis, position):
    parts = [value, shift(value, axis, 1), shift(value, axis, 2), shift(value, axis, -1)]
    shape = value.shape[:position] + (4,) + value.shape[position:]
    block = value.shape[:position] + (1,) + value.shape[position:]

    def out_index(i, me):
        return tuple((me[0] + i) % 4 if d == position else 0 for d in range(len(shape)))

    return pl.pallas_call(
        place_kernel,
        grid_spec=pltpu.PrefetchScalarGridSpec(
            num_scalar_prefetch=1,
            grid=(4,),
            in_specs=[pl.BlockSpec(value.shape, lambda i, me: (0,) * value.ndim)] * 4,
            out_specs=pl.BlockSpec(block, out_index),
        ),
        out_shape=jax.ShapeDtypeStruct(shape, value.dtype),
        compiler_params=pltpu.CompilerParams(vmem_limit_bytes=VMEM),
        name="place_" + axis,
    )(lax.axis_index(axis).reshape(1).astype(jnp.int32), *parts)


def gather_halves(a, b):
    pair_a, pair_b = gather_pair(a, "zl"), gather_pair(b, "zl")
    pair_a = pair_a.reshape(96, a.shape[1])
    pair_b = pair_b.reshape(96, b.shape[1])
    rows_a = gather_ring(pair_a, "x", 0)
    rows_b = gather_ring(pair_b, "y", 0)
    full_a = gather_ring(rows_a, "y", 0)
    full_b = gather_ring(rows_b, "x", 1)
    return full_a.reshape(1536, -1), full_b.reshape(1536, -1)


def scatter_ring(value, axis, position):
    me = lax.axis_index(axis)

    def entry(by):
        return lax.dynamic_index_in_dim(value, (me + by) % 4, position, keepdims=False)

    ahead = shift(entry(-1), axis, 1)
    behind = shift(entry(1), axis, -1)
    across = shift(entry(2), axis, 2)
    return (entry(0).astype(F32) + across.astype(F32)) + (ahead.astype(F32) + behind.astype(F32))


def scatter_pair(value, axis):
    me = lax.axis_index(axis)
    keep = lax.dynamic_index_in_dim(value, me, 0, keepdims=False)
    give = lax.dynamic_index_in_dim(value, 1 - me, 0, keepdims=False)
    return keep.astype(F32) + swap(give, axis).astype(F32)


def scatter_halves(a, b):
    blocks_a = a.reshape(4, 4, 96, a.shape[1])
    blocks_b = b.reshape(4, 4, 96, b.shape[1])
    half_a = scatter_ring(blocks_a, "y", 0).astype(BF16)
    half_b = scatter_ring(blocks_b, "x", 1).astype(BF16)
    mine_a = scatter_ring(half_a, "x", 0).astype(BF16)
    mine_b = scatter_ring(half_b, "y", 0).astype(BF16)
    both = jnp.concatenate([mine_a, mine_b], 1)
    return scatter_pair(both.reshape(2, 48, -1), "zl")


def sum_ring(value, axis):
    ahead, behind, across = shift(value, axis, 1), shift(value, axis, -1), shift(value, axis, 2)
    return (value + across) + (ahead + behind)


def sum_pair(value, axis):
    return value + swap(value, axis)


def gather_tokens(value):
    far = swap(value, "zh")
    near_pair = gather_pair(value, "c")
    far_pair = gather_pair(far, "c")
    both = ordered_pair(near_pair, far_pair, "zh")
    return both.reshape((4 * value.shape[0],) + value.shape[1:])


def scatter_tensor(value):
    by_zh = value.reshape((2, 2) + value.shape[1:])
    half = scatter_pair(jnp.swapaxes(by_zh, 0, 1), "c").astype(BF16)
    return scatter_pair(half, "zh")


def per_device(
    hidden_in,
    norm_gain,
    proj_zx,
    proj_shared,
    proj_step,
    conv_inner,
    conv_shared,
    step_bias,
    decay_log,
    skip_gain,
    gated_gain,
    proj_out,
    out_grad,
    segments,
):
    model_width = hidden_in.shape[1]
    width = proj_zx.shape[2]
    heads = step_bias.shape[0]
    cut = 640
    residual_in = hidden_in.astype(F32)
    scale_in = lax.rsqrt(jnp.mean(residual_in * residual_in, axis=-1, keepdims=True) + EPS)
    normed_low = (residual_in * scale_in * norm_gain).astype(BF16)

    shared_rows = gather_tokens(proj_shared)
    first_rows = jnp.concatenate(
        [proj_zx[:, 1, :], shared_rows, jnp.pad(proj_step, ((0, 0), (0, 128 - heads)))], 1
    )
    first_a, first_b = gather_halves(first_rows[:, :cut], first_rows[:, cut:])
    tokens = gather_tokens(normed_low)
    second_rows = jnp.concatenate([proj_zx[:, 0, :], proj_out.T], 1)
    second_full = lax.all_gather(gather_pair(second_rows, "zl"), ("y", "x"), axis=0, tiled=True)
    second_full = second_full.reshape(1536, 2 * width)
    gate_full = second_full[:, :width]
    out_full = second_full[:, width:]
    out_grad_late, tokens = lax.optimization_barrier((out_grad, tokens))
    grad_rows = gather_tokens(out_grad_late)

    pad = (0, 128 - heads)
    head_rows = jnp.stack([jnp.pad(step_bias, pad), jnp.pad(jnp.exp(decay_log), pad)], 0)
    head_rows = jnp.pad(head_rows, ((0, 6), (0, 0)))
    taps = jnp.pad(jnp.concatenate([conv_inner, conv_shared], 1), ((0, 3), (0, 0)))
    chan = jnp.broadcast_to(jnp.repeat(skip_gain, width // heads), (8, width))
    gain = jnp.broadcast_to(gated_gain, (8, width))
    marks, segrow = scan_marks(segments)
    pre, scanned, states = scan_forward(tokens, first_a, first_b, taps, head_rows, chan, marks, segrow)

    gate_pre, grad_mixed, sums = mix_first(tokens, grad_rows, gate_full, out_full, scanned, gain)
    sums = sum_pair(sum_pair(sums, "c"), "zh")
    mixed_low, projected, grad_scanned, gate_grad_low, gain_sums = mix_second(
        sums, gate_pre, grad_mixed, scanned, out_full, gain, 4 * width
    )
    mixed_sum = scatter_tensor(projected.reshape(4, -1, model_width))
    hidden_out = (residual_in + mixed_sum).astype(BF16)

    to_model = (((0,), (0,)), ((), ()))
    second_grad = jnp.concatenate(
        [
            lax.dot_general(tokens, gate_grad_low, to_model, preferred_element_type=F32).astype(BF16),
            lax.dot_general(grad_rows, mixed_low, to_model, preferred_element_type=F32).astype(BF16),
        ],
        1,
    )
    second_mine = lax.psum_scatter(second_grad, ("y", "x"), scatter_dimension=0, tiled=True)
    second_mine = scatter_pair(second_mine.reshape(2, 48, -1), "zl")
    grad_proj_gate = second_mine[:, :width]
    grad_proj_out = second_mine[:, width:].T

    sum_table = head_sum_table(width)
    low, tap_sums, head_sums = scan_backward(
        pre, taps, head_rows, chan, sum_table, marks, segrow, grad_scanned, states
    )
    token_rows, gain_in = token_grads(tokens, gate_grad_low, low, gate_full, first_a, first_b)
    grad_gain_in = gain_in[0] / norm_gain
    grad_normed = scatter_tensor(token_rows.reshape(4, -1, model_width))
    weighted = jnp.sum(grad_normed * norm_gain * residual_in, axis=-1, keepdims=True)
    grad_hidden = (
        out_grad.astype(F32)
        + scale_in * norm_gain * grad_normed
        - residual_in * scale_in**3 * weighted / model_width
    ).astype(BF16)

    first_grad = lax.dot_general(tokens, low, to_model, preferred_element_type=F32).astype(BF16)
    shared_parts = first_grad[:, width : width + 256].reshape(32, 4, 12, 256).swapaxes(0, 1)
    shared_part = scatter_tensor(shared_parts).astype(BF16).reshape(1536, 64)
    rest = jnp.concatenate(
        [first_grad[:, 512:width], shared_part, first_grad[:, width + 256 : width + 256 + 64]], 1
    )
    first_mine = scatter_halves(first_grad[:, :512], rest)
    grad_proj_inner = first_mine[:, :width]
    grad_proj_shared = first_mine[:, width : width + 64].reshape(12, 256)
    grad_proj_step = first_mine[:, width + 64 : width + 64 + heads]
    grad_proj_zx = jnp.stack([grad_proj_gate, grad_proj_inner], 1)

    everywhere = jnp.concatenate([grad_gain_in, tap_sums[:5, width:].reshape(-1)])
    everywhere = sum_pair(sum_pair(everywhere, "c"), "zh")
    small = jnp.concatenate(
        [everywhere, tap_sums[:5, :width].reshape(-1), gain_sums[0], head_sums[:3, :heads].reshape(-1)]
    )
    count = small.shape[0]
    small = jnp.pad(small, (0, 8192 - count)).reshape(8, 1024)
    small = sum_pair(sum_ring(sum_ring(small, "y"), "x"), "zl").reshape(-1)
    cuts = [model_width, 5 * 256, 5 * width, width, heads, heads, heads]
    parts, place = [], 0
    for size in cuts:
        parts.append(small[place : place + size])
        place += size
    return (
        hidden_out,
        grad_hidden,
        parts[0],
        grad_proj_zx,
        grad_proj_shared,
        grad_proj_step,
        parts[2].reshape(5, width),
        parts[1].reshape(5, 256),
        parts[4],
        parts[5],
        parts[6],
        parts[3],
        grad_proj_out,
    )


def solution(mesh):
    fine = Mesh(mesh.devices.reshape(4, 4, 2, 2, 2), DP + TENSOR)
    both = DP + TENSOR
    return jax.shard_map(
        per_device,
        mesh=fine,
        in_specs=(
            P(both, None),
            P(),
            P(DP, None, TENSOR),
            P(both, None),
            P(DP, TENSOR),
            P(None, TENSOR),
            P(),
            P(TENSOR),
            P(TENSOR),
            P(TENSOR),
            P(TENSOR),
            P(TENSOR, DP),
            P(both, None),
            P(DP),
        ),
        out_specs=(
            P(both, None),
            P(both, None),
            P(),
            P(DP, None, TENSOR),
            P(both, None),
            P(DP, TENSOR),
            P(None, TENSOR),
            P(),
            P(TENSOR),
            P(TENSOR),
            P(TENSOR),
            P(TENSOR),
            P(TENSOR, DP),
        ),
        check_vma=False,
    )
```

time: 914 us -> 395 us (0.43); the launches traced: 898 us -> 389 us
  local copies, waits for them, and re-layouts: 336 us -> 39.6 us
  matrix products: 171 us -> 12 us
  other arithmetic: 148 us -> 28.2 us
  Pallas kernels: 0 us -> 95.2 us
  waiting for transfers between devices: 172 us -> 117 us
  starting transfers between devices: 62.9 us -> 81.7 us
  between operations: 2.74 us -> 15.3 us
    dynamic_update_slice x44 -> x0, local copies, waits for them, and re-layouts: 170 us -> none  [block_mixer(): lax.scan(advance, initial, (inner_blocks, write_blocks, read_blocks, step...]
    dot_general x51 -> x1, matrix products: 157 us -> 4.55 us  [per_device(): lax.dot_general(tokens, low, to_model, preferred_element_type=F32)]
    pallas_call x0 -> x9, Pallas kernels: none -> 95.2 us  [the longest x1 30.4 us: scan_backward(): pl.pallas_call(scan_backward_kernel, grid=(blocks,), in_specs=[pl.BlockSp...]
    ppermute x54 -> x55, waiting for transfers between devices: 172 us -> 117 us  [shift(): return lax.ppermute(value, axis, [(i, (i - by) % n) for i in range(n)])]
    dynamic_update_slice x24 -> x0, other arithmetic: 40.5 us -> none  [block_mixer(): lax.scan(advance, initial, (inner_blocks, write_blocks, read_blocks, step...]
    unnamed x235 -> x85, local copies, waits for them, and re-layouts: 47.9 us -> 12 us
    dynamic_slice x18 -> x0, local copies, waits for them, and re-layouts: 26.2 us -> none  [the longest x16 20.9 us: block_mixer(): lax.scan(advance, initial, (inner_blocks, write_blocks, read_blocks, step...]
    reduce_sum x11 -> x0, other arithmetic: 22.3 us -> none  [the longest x2 11.9 us: causal_conv(): conv_taps[offset] * jnp.where(same_doc, padded[offset:offset + length], 0.0)]
  transfers between devices with their start and end apart: 54 -> 57, of which waited for: 23 -> 24; matrix products, arithmetic and copies ran while one was open for 38% -> 12% of each run, Pallas kernels for 0% -> 19%
where the time goes in v2:
time: 395 us; the launch traced here: 389 us
  waiting for transfers between devices  117 us (30%)
  Pallas kernels  95.2 us (24%)
  starting transfers between devices  81.7 us (21%)
  local copies, waits for them, and re-layouts  39.6 us (10%)
  other arithmetic  28.2 us (7%)
  between operations  15.3 us (4%)
  matrix products  12 us (3%)
    ppermute x55, waiting for transfers between devices, shift(): return lax.ppermute(value, axis, [(i, (i - by) % n) for i in range(n)])  117 us
    ppermute x55, starting transfers between devices, shift(): return lax.ppermute(value, axis, [(i, (i - by) % n) for i in range(n)])  81.6 us
    pallas_call x1, Pallas kernels, scan_backward(): pl.pallas_call(scan_backward_kernel, grid=(blocks,), in_specs=[pl.BlockSp...  30.4 us
    pallas_call x1, Pallas kernels, scan_forward(): pl.pallas_call(scan_forward_kernel, grid=(blocks,), in_specs=[pl.BlockSpe...  19.9 us
    pallas_call x1, Pallas kernels, token_grads(): pl.pallas_call(token_grads_kernel, grid=(length // n,), in_specs=[rows(mo...  12.1 us
    unnamed x85, local copies, waits for them, and re-layouts  12 us
    pallas_call x4, Pallas kernels, gather_ring(): pl.pallas_call(place_kernel, grid_spec=pltpu.PrefetchScalarGridSpec(num_s...  11.3 us
    pallas_call x1, Pallas kernels, mix_second(): pl.pallas_call(lambda *refs: mix_second_kernel(channels, *refs), grid=(le...  11.1 us
  transfers between devices with their start and end apart: 57, of which 24 were waited for; matrix products, arithmetic and copies ran while one was open for 12% of the time, Pallas kernels for 19%

profile of v2, /device:TPU:24, one launch (start us, length us, event | category | flops | bytes accessed | tf_op | source)
XLA Modules:
  0.0 389.0 jit_solution(429625712850614833)
XLA Ops:
  11.5 3.8 collective-permute-done.6
  17.1 3.8 collective-permute-start.15
  25.9 17.5 %collective-permute-done.17 = bf16[48,512]{1,0:T(8,128)(2,1)S(1)} collective-permute-done((bf16[48,512]{1,0:T(8,128)(2,1)S(1)}, bf16[48,512]{1,0:T(8,128)(2,1)S(1)}, u32[]{:S(2)}, u32[]{:S(2)}) %collective-permute-start.17) | collective-permute-done | bytes 49184 | tf_op jit(solution)/shard_map/ppermute | solution.py:499
  54.9 3.7 collective-permute-start.4
  72.0 12.5 %collective-permute-done.21.refs_1_ = bf16[4,96,512]{2,1,0:T(8,128)(2,1)S(1)} collective-permute-done((bf16[4,96,512]{2,1,0:T(8,128)(2,1)}, bf16[4,96,512]{2,1,0:T(8,128)(2,1)S(1)}, u32[]{:S(2)}, u32[]{:S(2)}) %collective-permute-start.21) | collective-permute-done | bytes 393248 | tf_op jit(solution)/shard_map/ppermute | solution.py:499
  88.5 5.3 %collective-permute-done.23.refs_3_ = bf16[4,96,512]{2,1,0:T(8,128)(2,1)} collective-permute-done((bf16[4,96,512]{2,1,0:T(8,128)(2,1)}, bf16[4,96,512]{2,1,0:T(8,128)(2,1)}, u32[]{:S(2)}, u32[]{:S(2)}) %collective-permute-start.23) | collective-permute-done | bytes 393248 | tf_op jit(solution)/shard_map/ppermute | solution.py:499
  97.8 3.1 place_x.3
  100.8 7.3 %collective-permute-done.11.refs_1_ = bf16[4,96,640]{2,1,0:T(8,128)(2,1)S(1)} collective-permute-done((bf16[4,96,640]{2,1,0:T(8,128)(2,1)}, bf16[4,96,640]{2,1,0:T(8,128)(2,1)S(1)}, u32[]{:S(2)}, u32[]{:S(2)}) %collective-permute-start.11) | collective-permute-done | bytes 491552 | tf_op jit(solution)/shard_map/ppermute | solution.py:499
  108.9 3.4 place_y.2
  113.5 19.9 %scan_forward.1 = (f32[1024,1152]{1,0:T(8,128)}, f32[1024,768]{1,0:T(8,128)}, bf16[8,128,768]{2,1,0:T(8,128)(2,1)}) custom-call(bf16[1024,1536]{1,0:T(8,128)(2,1)} %bitcast.185, bf16[1536,640]{1,0:T(8,128)(2,1)} %bitcast.190, bf16[1536,512]{1,0:T(8,128)(2,1)} %bitcast.192, f32[8,1024]{1,0:T(8,128)} %select_maximum_fusion.3.taps, ...), custom_call_target="tpu_custom_call" | custom-call | tf_op jit(solution)/shard_map/scan_forward/pallas_call | solution.py:276
  137.1 4.9 %fusion.32 = (bf16[1536,768]{1,0:T(8,128)(2,1)}, bf16[1536,768]{1,0:T(8,128)(2,1)}) fusion(bf16[1536,1536]{1,0:T(8,128)(2,1)} %bitcast.198), kind=kLoop, calls=%fused_computation.157 | loop fusion | bytes 9437184 | tf_op jit(solution)/shard_map/slice | solution.py:643
  142.6 10.5 %mix_first.1 = (f32[1024,768]{1,0:T(8,128)}, f32[1024,768]{1,0:T(8,128)}, f32[8,1024]{1,0:T(8,128)}) custom-call(bf16[1024,1536]{1,0:T(8,128)(2,1)} %bitcast.186, bf16[1024,1536]{1,0:T(8,128)(2,1)} %bitcast.194, bf16[1536,768]{1,0:T(8,128)(2,1)} %get-tuple-element.102.gate_w, bf16[1536,768]{1,0:T(8,128)(2,1)} %get-tuple-element.101.out_w.refs_4_, ...), custom_call_target="tpu_custom_call" | custom-call | tf_op jit(solution)/shard_map/mix_first/pallas_call | solution.py:394
  156.1 4.6 %collective-permute-done.25 = f32[8,1024]{1,0:T(8,128)S(1)} collective-permute-done((f32[8,1024]{1,0:T(8,128)S(1)}, f32[8,1024]{1,0:T(8,128)S(1)}, u32[]{:S(2)}, u32[]{:S(2)}) %collective-permute-start.25) | collective-permute-done | bytes 32800 | tf_op jit(solution)/shard_map/ppermute | solution.py:499
  161.4 11.1 %mix_second.1 = (bf16[1024,768]{1,0:T(8,128)(2,1)}, bf16[1024,1536]{1,0:T(8,128)(2,1)}, f32[1024,768]{1,0:T(8,128)}, bf16[1024,768]{1,0:T(8,128)(2,1)}, f32[8,768]{1,0:T(8,128)}) custom-call(f32[8,1024]{1,0:T(8,128)} %add.297.refs_0_, f32[1024,768]{1,0:T(8,128)} %get-tuple-element.35.refs_1_, f32[1024,768]{1,0:T(8,128)} %get-tuple-element.36.refs_2_, ...), custom_call_target="tpu_custom_call" | custom-call | tf_op jit(solution)/shard_map/mix_second/pallas_call | solution.py:446
  172.5 4.5 %convolution_convert_fusion.1 = bf16[1536,768]{0,1:T(8,128)(2,1)S(1)} fusion(bf16[1024,1536]{1,0:T(8,128)(2,1)S(1)} %bitcast.195, bf16[1024,768]{1,0:T(8,128)(2,1)} %get-tuple-element.48), kind=kOutput, calls=%fused_computation.2 | convolution fusion | flops 2417098752 | bytes 7077888 | tf_op jit(solution)/shard_map/dot_general | solution.py:668
  177.0 2.9 convolution_convert_fusion.2
  182.5 6.7 %copy.84 = bf16[1536,1536]{1,0:T(8,128)(2,1)} copy(bf16[1536,1536]{0,1:T(8,128)(2,1)} %pad_maximum_fusion) | data formatting | bytes 9437184
  190.4 30.4 %scan_backward.1 = (bf16[1024,1152]{1,0:T(8,128)(2,1)}, f32[8,1024]{1,0:T(8,128)}, f32[8,128]{1,0:T(8,128)}) custom-call(f32[1024,1152]{1,0:T(8,128)} %get-tuple-element.39.pre.pre_before, f32[1024,1152]{1,0:T(8,128)} %get-tuple-element.39.pre.pre_before, f32[8,1024]{1,0:T(8,128)} %select_maximum_fusion.3.taps, f32[8,128]{1,0:T(8,128)} %select_maximum_fusion.4.heads, ...), custom_call_target="tpu_custom_call" | custom-call | tf_op jit(solution)/shard_map/scan_backward/pallas_call | solution.py:323
  220.8 12.1 %token_grads.1 = (bf16[1024,1536]{1,0:T(8,128)(2,1)}, f32[8,1536]{1,0:T(8,128)}) custom-call(bf16[1024,1536]{1,0:T(8,128)(2,1)} %bitcast.187, bf16[1024,768]{1,0:T(8,128)(2,1)} %get-tuple-element.38.grad_gate, bf16[1024,1152]{1,0:T(8,128)(2,1)} %get-tuple-element.42.low, bf16[1536,768]{1,0:T(8,128)(2,1)} %get-tuple-element.102.gate_w, ...), custom_call_target="tpu_custom_call" | custom-call | tf_op jit(solution)/shard_map/token_grads/pallas_call | solution.py:486
  232.9 4.6 %convolution_convert_fusion = bf16[1536,1152]{1,0:T(8,128)(2,1)S(1)} fusion(bf16[1024,1536]{1,0:T(8,128)(2,1)S(1)} %bitcast.189, bf16[1024,1152]{1,0:T(8,128)(2,1)S(1)} %copy-done.13), kind=kOutput, calls=%fused_computation | convolution fusion | flops 3625648128 | bytes 9043968 | tf_op jit(solution)/shard_map/dot_general | solution.py:691
  240.5 10.3 %collective-permute-start.30 = (f32[2816]{0:T(1024)S(1)}, f32[2816]{0:T(1024)S(1)}, u32[]{:S(2)}, u32[]{:S(2)}) collective-permute-start(f32[2816]{0:T(1024)S(1)} %pad_maximum_fusion.18), channel_id=1, source_target_pairs={{0,1},{1,0},{2,3},{3,2},{4,5},{5,4},{6,7},{7,6},{8,9},{9,8},{10,11... | collective-permute-start | bytes 33800 | tf_op jit(solution)/shard_map/ppermute | solution.py:499
  254.9 3.5 collective-permute-done.31
  268.8 11.8 %collective-permute-start.36 = (f32[8,1024]{1,0:T(8,128)S(1)}, f32[8,1024]{1,0:T(8,128)S(1)}, u32[]{:S(2)}, u32[]{:S(2)}) collective-permute-start(f32[8,1024]{1,0:T(8,128)S(1)} %add_add_fusion.1), channel_id=1, source_target_pairs={{0,24},{8,0},{16,8},{24,16},{1,25},{9,1},{17,9},{25,17},{2,26},{10... | collective-permute-start | bytes 98312 | tf_op jit(solution)/shard_map/ppermute | solution.py:499
  282.2 3.5 collective-permute-done.37
  296.0 3.1 collective-permute-start.47
  299.7 6.6 %collective-permute-done.47 = bf16[32,12,256]{2,1,0:T(8,128)(2,1)S(1)} collective-permute-done((bf16[32,12,256]{2,1,0:T(8,128)(2,1)S(1)}, bf16[32,12,256]{2,1,0:T(8,128)(2,1)S(1)}, u32[]{:S(2)}, u32[]{:S(2)}) %collective-permute-start.47) | collective-permute-done | bytes 196640 | tf_op jit(solution)/shard_map/ppermute | solution.py:499
  310.7 7.7 %collective-permute-done.48 = bf16[4,96,384]{2,1,0:T(8,128)(2,1)S(1)} collective-permute-done((bf16[4,96,384]{2,1,0:T(8,128)(2,1)S(1)}, bf16[4,96,384]{2,1,0:T(8,128)(2,1)S(1)}, u32[]{:S(2)}, u32[]{:S(2)}) %collective-permute-start.48) | collective-permute-done | bytes 294944 | tf_op jit(solution)/shard_map/ppermute | solution.py:499
  318.5 3.6 collective-permute-done.49
  338.5 3.2 collective-permute-start.29
  347.4 13.3 %collective-permute-done.29 = bf16[256,1536]{1,0:T(8,128)(2,1)S(1)} collective-permute-done((bf16[256,1536]{1,0:T(8,128)(2,1)}, bf16[256,1536]{1,0:T(8,128)(2,1)S(1)}, u32[]{:S(2)}, u32[]{:S(2)}) %collective-permute-start.29) | collective-permute-done | bytes 786464 | tf_op jit(solution)/shard_map/ppermute | solution.py:499
  363.7 13.0 %collective-permute-done.27 = bf16[256,1536]{1,0:T(8,128)(2,1)} collective-permute-done((bf16[256,1536]{1,0:T(8,128)(2,1)}, bf16[256,1536]{1,0:T(8,128)(2,1)}, u32[]{:S(2)}, u32[]{:S(2)}) %collective-permute-start.27) | collective-permute-done | bytes 786464 | tf_op jit(solution)/shard_map/ppermute | solution.py:499
  376.6 3.7 fusion.9
  (298 shorter events, 118.1 us)
Async XLA Ops:
  7.2 129.9 %all-gather.2.cloned.1.call-start = ((), (), s32[]{:S(2)}) async-start(), calls=%async_computation.1 | async-start | bytes 5013504 | tf_op jit(solution)/shard_map/all_gather | solution.py:640
  17.0 344.1 %reduce-scatter.4.cloned.1.call-start = ((), (), s32[]{:S(2)}) async-start(), calls=%async_computation.2 | async-start | bytes 5013504 | tf_op jit(solution)/shard_map/reduce_scatter | solution.py:672
  21.4 25.9 %collective-permute-start.1 = (bf16[256,1536]{1,0:T(8,128)(2,1)S(1)}, bf16[256,1536]{1,0:T(8,128)(2,1)S(1)}, u32[]{:S(2)}, u32[]{:S(2)}) collective-permute-start(bf16[256,1536]{1,0:T(8,128)(2,1)S(1)} %fusion.4), channel_id=1, source_target_pairs={{0,2},{2,0},{1,3},{3,1},{4,6},{6,4},{5,7},{7,5},{8,10},{10,8},{9,1... | collective-permute-start | bytes 2359304 | tf_op jit(solution)/shard_map/ppermute | solution.py:499
  21.6 26.6 %collective-permute-start = (bf16[256,1536]{1,0:T(8,128)(2,1)S(1)}, bf16[256,1536]{1,0:T(8,128)(2,1)S(1)}, u32[]{:S(2)}, u32[]{:S(2)}) collective-permute-start(bf16[256,1536]{1,0:T(8,128)(2,1)S(1)} %fusion.4), channel_id=1, source_target_pairs={{0,1},{1,0},{2,3},{3,2},{4,5},{5,4},{6,7},{7,6},{8,9},{9,8},{10,11... | collective-permute-start | bytes 2359304 | tf_op jit(solution)/shard_map/ppermute | solution.py:499
  22.1 23.0 %collective-permute-start.7 = (bf16[48,640]{1,0:T(8,128)(2,1)S(1)}, bf16[48,640]{1,0:T(8,128)(2,1)}, u32[]{:S(2)}, u32[]{:S(2)}) collective-permute-start(bf16[48,640]{1,0:T(8,128)(2,1)S(1)} %slice.146), channel_id=1, source_target_pairs={{0,4},{4,0},{1,5},{5,1},{2,6},{6,2},{3,7},{7,3},{8,12},{12,8},{9,1... | collective-permute-start | bytes 184328 | tf_op jit(solution)/shard_map/ppermute | solution.py:499
  24.9 18.5 %collective-permute-start.17 = (bf16[48,512]{1,0:T(8,128)(2,1)S(1)}, bf16[48,512]{1,0:T(8,128)(2,1)S(1)}, u32[]{:S(2)}, u32[]{:S(2)}) collective-permute-start(bf16[48,512]{1,0:T(8,128)(2,1)S(1)} %fusion.23), channel_id=1, source_target_pairs={{0,4},{4,0},{1,5},{5,1},{2,6},{6,2},{3,7},{7,3},{8,12},{12,8},{9,1... | collective-permute-start | bytes 147464 | tf_op jit(solution)/shard_map/ppermute | solution.py:499
  44.2 14.5 %collective-permute-start.19 = (bf16[96,512]{1,0:T(8,128)(2,1)S(1)}, bf16[96,512]{1,0:T(8,128)(2,1)S(1)}, u32[]{:S(2)}, u32[]{:S(2)}) collective-permute-start(bf16[96,512]{1,0:T(8,128)(2,1)S(1)} %bitcast.220), channel_id=1, source_target_pairs={{0,64},{32,96},{64,0},{96,32},{1,65},{33,97},{65,1},{97,33},{2,66}... | collective-permute-start | bytes 294920 | tf_op jit(solution)/shard_map/ppermute | solution.py:499
  45.1 15.2 %collective-permute-start.20 = (bf16[96,512]{1,0:T(8,128)(2,1)S(1)}, bf16[96,512]{1,0:T(8,128)(2,1)S(1)}, u32[]{:S(2)}, u32[]{:S(2)}) collective-permute-start(bf16[96,512]{1,0:T(8,128)(2,1)S(1)} %bitcast.221), channel_id=1, source_target_pairs={{0,32},{32,64},{64,96},{96,0},{1,33},{33,65},{65,97},{97,1},{2,34}... | collective-permute-start | bytes 294920 | tf_op jit(solution)/shard_map/ppermute | solution.py:499
  48.2 16.3 %collective-permute-start.10 = (bf16[96,640]{1,0:T(8,128)(2,1)S(1)}, bf16[96,640]{1,0:T(8,128)(2,1)S(1)}, u32[]{:S(2)}, u32[]{:S(2)}) collective-permute-start(bf16[96,640]{1,0:T(8,128)(2,1)S(1)} %bitcast.213), channel_id=1, source_target_pairs={{0,8},{8,16},{16,24},{24,0},{1,9},{9,17},{17,25},{25,1},{2,10},{10... | collective-permute-start | bytes 368648 | tf_op jit(solution)/shard_map/ppermute | solution.py:499
  50.3 15.7 %collective-permute-start.8 = (bf16[96,640]{1,0:T(8,128)(2,1)S(1)}, bf16[96,640]{1,0:T(8,128)(2,1)S(1)}, u32[]{:S(2)}, u32[]{:S(2)}) collective-permute-start(bf16[96,640]{1,0:T(8,128)(2,1)S(1)} %bitcast.214), channel_id=1, source_target_pairs={{0,24},{8,0},{16,8},{24,16},{1,25},{9,1},{17,9},{25,17},{2,26},{10... | collective-permute-start | bytes 368648 | tf_op jit(solution)/shard_map/ppermute | solution.py:499
  54.9 40.0 %collective-permute-start.4 = (bf16[256,1536]{1,0:T(8,128)(2,1)S(1)}, bf16[256,1536]{1,0:T(8,128)(2,1)S(1)}, u32[]{:S(2)}, u32[]{:S(2)}) collective-permute-start(bf16[256,1536]{1,0:T(8,128)(2,1)S(1)} %copy-done.11), channel_id=1, source_target_pairs={{0,2},{2,0},{1,3},{3,1},{4,6},{6,4},{5,7},{7,5},{8,10},{10,8},{9,1... | collective-permute-start | bytes 2359304 | tf_op jit(solution)/shard_map/ppermute | solution.py:499
  63.4 21.2 %collective-permute-start.21 = (bf16[4,96,512]{2,1,0:T(8,128)(2,1)}, bf16[4,96,512]{2,1,0:T(8,128)(2,1)S(1)}, u32[]{:S(2)}, u32[]{:S(2)}) collective-permute-start(bf16[4,96,512]{2,1,0:T(8,128)(2,1)} %place_y.3.refs_0_), channel_id=1, source_target_pairs={{0,24},{8,0},{16,8},{24,16},{1,25},{9,1},{17,9},{25,17},{2,26},{10... | collective-permute-start | bytes 1179656 | tf_op jit(solution)/shard_map/ppermute | solution.py:499
  64.5 22.2 %collective-permute-start.22 = (bf16[4,96,512]{2,1,0:T(8,128)(2,1)}, bf16[4,96,512]{2,1,0:T(8,128)(2,1)}, u32[]{:S(2)}, u32[]{:S(2)}) collective-permute-start(bf16[4,96,512]{2,1,0:T(8,128)(2,1)} %place_y.3.refs_0_), channel_id=1, source_target_pairs={{0,16},{8,24},{16,0},{24,8},{1,17},{9,25},{17,1},{25,9},{2,18},{10... | collective-permute-start | bytes 1179656 | tf_op jit(solution)/shard_map/ppermute | solution.py:499
  66.0 27.8 %collective-permute-start.23 = (bf16[4,96,512]{2,1,0:T(8,128)(2,1)}, bf16[4,96,512]{2,1,0:T(8,128)(2,1)}, u32[]{:S(2)}, u32[]{:S(2)}) collective-permute-start(bf16[4,96,512]{2,1,0:T(8,128)(2,1)} %place_y.3.refs_0_), channel_id=1, source_target_pairs={{0,8},{8,16},{16,24},{24,0},{1,9},{9,17},{17,25},{25,1},{2,10},{10... | collective-permute-start | bytes 1179656 | tf_op jit(solution)/shard_map/ppermute | solution.py:499
  68.9 64.5 %collective-permute-start.3 = (bf16[256,1536]{1,0:T(8,128)(2,1)S(1)}, bf16[256,1536]{1,0:T(8,128)(2,1)S(1)}, u32[]{:S(2)}, u32[]{:S(2)}) collective-permute-start(bf16[256,1536]{1,0:T(8,128)(2,1)S(1)} %copy-done.11), channel_id=1, source_target_pairs={{0,1},{1,0},{2,3},{3,2},{4,5},{5,4},{6,7},{7,6},{8,9},{9,8},{10,11... | collective-permute-start | bytes 2359304 | tf_op jit(solution)/shard_map/ppermute | solution.py:499
  84.5 23.6 %collective-permute-start.11 = (bf16[4,96,640]{2,1,0:T(8,128)(2,1)}, bf16[4,96,640]{2,1,0:T(8,128)(2,1)S(1)}, u32[]{:S(2)}, u32[]{:S(2)}) collective-permute-start(bf16[4,96,640]{2,1,0:T(8,128)(2,1)} %place_x.2.refs_0_), channel_id=1, source_target_pairs={{0,96},{32,0},{64,32},{96,64},{1,97},{33,1},{65,33},{97,65},{2,98}... | collective-permute-start | bytes 1474568 | tf_op jit(solution)/shard_map/ppermute | solution.py:499
  86.7 21.4 %collective-permute-start.12 = (bf16[4,96,640]{2,1,0:T(8,128)(2,1)}, bf16[4,96,640]{2,1,0:T(8,128)(2,1)}, u32[]{:S(2)}, u32[]{:S(2)}) collective-permute-start(bf16[4,96,640]{2,1,0:T(8,128)(2,1)} %place_x.2.refs_0_), channel_id=1, source_target_pairs={{0,64},{32,96},{64,0},{96,32},{1,65},{33,97},{65,1},{97,33},{2,66}... | collective-permute-start | bytes 1474568 | tf_op jit(solution)/shard_map/ppermute | solution.py:499
  93.8 15.0 %collective-permute-start.13 = (bf16[4,96,640]{2,1,0:T(8,128)(2,1)}, bf16[4,96,640]{2,1,0:T(8,128)(2,1)}, u32[]{:S(2)}, u32[]{:S(2)}) collective-permute-start(bf16[4,96,640]{2,1,0:T(8,128)(2,1)} %place_x.2.refs_0_), channel_id=1, source_target_pairs={{0,32},{32,64},{64,96},{96,0},{1,33},{33,65},{65,97},{97,1},{2,34}... | collective-permute-start | bytes 1474568 | tf_op jit(solution)/shard_map/ppermute | solution.py:499
  94.9 38.7 %collective-permute-start.5 = (bf16[256,1536]{1,0:T(8,128)(2,1)S(1)}, bf16[256,1536]{1,0:T(8,128)(2,1)}, u32[]{:S(2)}, u32[]{:S(2)}) collective-permute-start(bf16[256,1536]{1,0:T(8,128)(2,1)S(1)} %collective-permute-done.4), channel_id=1, source_target_pairs={{0,1},{1,0},{2,3},{3,2},{4,5},{5,4},{6,7},{7,6},{8,9},{9,8},{10,11... | collective-permute-start | bytes 2359304 | tf_op jit(solution)/shard_map/ppermute | solution.py:499
  252.6 42.0 %collective-permute-start.46 = (bf16[2,32,12,256]{3,2,1,0:T(8,128)(2,1)}, bf16[2,32,12,256]{3,2,1,0:T(8,128)(2,1)}, u32[]{:S(2)}, u32[]{:S(2)}) collective-permute-start(bf16[2,32,12,256]{3,2,1,0:T(8,128)(2,1)} %bitcast.181), channel_id=1, source_target_pairs={{0,1},{1,0},{2,3},{3,2},{4,5},{5,4},{6,7},{7,6},{8,9},{9,8},{10,11... | collective-permute-start | bytes 1179656 | tf_op jit(solution)/shard_map/ppermute | solution.py:499
  266.7 15.4 %collective-permute-start.35 = (f32[8,1024]{1,0:T(8,128)S(1)}, f32[8,1024]{1,0:T(8,128)S(1)}, u32[]{:S(2)}, u32[]{:S(2)}) collective-permute-start(f32[8,1024]{1,0:T(8,128)S(1)} %add_add_fusion.1), channel_id=1, source_target_pairs={{0,16},{8,24},{16,0},{24,8},{1,17},{9,25},{17,1},{25,9},{2,18},{10... | collective-permute-start | bytes 98312 | tf_op jit(solution)/shard_map/ppermute | solution.py:499
  268.8 13.4 %collective-permute-start.36 = (f32[8,1024]{1,0:T(8,128)S(1)}, f32[8,1024]{1,0:T(8,128)S(1)}, u32[]{:S(2)}, u32[]{:S(2)}) collective-permute-start(f32[8,1024]{1,0:T(8,128)S(1)} %add_add_fusion.1), channel_id=1, source_target_pairs={{0,24},{8,0},{16,8},{24,16},{1,25},{9,1},{17,9},{25,17},{2,26},{10... | collective-permute-start | bytes 98312 | tf_op jit(solution)/shard_map/ppermute | solution.py:499
  288.1 18.9 %collective-permute-start.40 = (bf16[4,96,512]{2,1,0:T(8,128)(2,1)}, bf16[4,96,512]{2,1,0:T(8,128)(2,1)}, u32[]{:S(2)}, u32[]{:S(2)}) collective-permute-start(bf16[4,96,512]{2,1,0:T(8,128)(2,1)} %get-tuple-element.109), channel_id=1, source_target_pairs={{0,64},{32,96},{64,0},{96,32},{1,65},{33,97},{65,1},{97,33},{2,66}... | collective-permute-start | bytes 1179656 | tf_op jit(solution)/shard_map/ppermute | solution.py:499
  289.0 18.1 %collective-permute-start.41 = (bf16[4,96,512]{2,1,0:T(8,128)(2,1)}, bf16[4,96,512]{2,1,0:T(8,128)(2,1)}, u32[]{:S(2)}, u32[]{:S(2)}) collective-permute-start(bf16[4,96,512]{2,1,0:T(8,128)(2,1)} %get-tuple-element.111), channel_id=1, source_target_pairs={{0,96},{32,0},{64,32},{96,64},{1,97},{33,1},{65,33},{97,65},{2,98}... | collective-permute-start | bytes 1179656 | tf_op jit(solution)/shard_map/ppermute | solution.py:499
  291.2 17.3 %collective-permute-start.42 = (bf16[4,96,512]{2,1,0:T(8,128)(2,1)}, bf16[4,96,512]{2,1,0:T(8,128)(2,1)}, u32[]{:S(2)}, u32[]{:S(2)}) collective-permute-start(bf16[4,96,512]{2,1,0:T(8,128)(2,1)} %get-tuple-element.110), channel_id=1, source_target_pairs={{0,32},{32,64},{64,96},{96,0},{1,33},{33,65},{65,97},{97,1},{2,34}... | collective-permute-start | bytes 1179656 | tf_op jit(solution)/shard_map/ppermute | solution.py:499
  292.2 49.4 %collective-permute-start.26 = (bf16[2,256,1536]{2,1,0:T(8,128)(2,1)}, bf16[2,256,1536]{2,1,0:T(8,128)(2,1)}, u32[]{:S(2)}, u32[]{:S(2)}) collective-permute-start(bf16[2,256,1536]{2,1,0:T(8,128)(2,1)} %dynamic-slice_bitcast_fusion.1), channel_id=1, source_target_pairs={{0,1},{1,0},{2,3},{3,2},{4,5},{5,4},{6,7},{7,6},{8,9},{9,8},{10,11... | collective-permute-start | bytes 4718600 | tf_op jit(solution)/shard_map/ppermute | solution.py:499
  306.3 29.3 %collective-permute-start.28 = (bf16[2,256,1536]{2,1,0:T(8,128)(2,1)}, bf16[2,256,1536]{2,1,0:T(8,128)(2,1)}, u32[]{:S(2)}, u32[]{:S(2)}) collective-permute-start(bf16[2,256,1536]{2,1,0:T(8,128)(2,1)} %dynamic-slice_bitcast_fusion), channel_id=1, source_target_pairs={{0,1},{1,0},{2,3},{3,2},{4,5},{5,4},{6,7},{7,6},{8,9},{9,8},{10,11... | collective-permute-start | bytes 4718600 | tf_op jit(solution)/shard_map/ppermute | solution.py:499
  307.1 15.0 %collective-permute-start.49 = (bf16[4,96,384]{2,1,0:T(8,128)(2,1)S(1)}, bf16[4,96,384]{2,1,0:T(8,128)(2,1)S(1)}, u32[]{:S(2)}, u32[]{:S(2)}) collective-permute-start(bf16[4,96,384]{2,1,0:T(8,128)(2,1)S(1)} %get-tuple-element.122), channel_id=1, source_target_pairs={{0,24},{8,0},{16,8},{24,16},{1,25},{9,1},{17,9},{25,17},{2,26},{10... | collective-permute-start | bytes 884744 | tf_op jit(solution)/shard_map/ppermute | solution.py:499
  308.6 16.1 %collective-permute-start.50 = (bf16[4,96,384]{2,1,0:T(8,128)(2,1)S(1)}, bf16[4,96,384]{2,1,0:T(8,128)(2,1)S(1)}, u32[]{:S(2)}, u32[]{:S(2)}) collective-permute-start(bf16[4,96,384]{2,1,0:T(8,128)(2,1)S(1)} %get-tuple-element.121), channel_id=1, source_target_pairs={{0,8},{8,16},{16,24},{24,0},{1,9},{9,17},{17,25},{25,1},{2,10},{10... | collective-permute-start | bytes 884744 | tf_op jit(solution)/shard_map/ppermute | solution.py:499
  338.5 22.2 %collective-permute-start.29 = (bf16[256,1536]{1,0:T(8,128)(2,1)}, bf16[256,1536]{1,0:T(8,128)(2,1)S(1)}, u32[]{:S(2)}, u32[]{:S(2)}) collective-permute-start(bf16[256,1536]{1,0:T(8,128)(2,1)} %dynamic-slice_bitcast_fusion.2), channel_id=1, source_target_pairs={{0,2},{2,0},{1,3},{3,1},{4,6},{6,4},{5,7},{7,5},{8,10},{10,8},{9,1... | collective-permute-start | bytes 2359304 | tf_op jit(solution)/shard_map/ppermute | solution.py:499
  345.5 31.1 %collective-permute-start.27 = (bf16[256,1536]{1,0:T(8,128)(2,1)}, bf16[256,1536]{1,0:T(8,128)(2,1)}, u32[]{:S(2)}, u32[]{:S(2)}) collective-permute-start(bf16[256,1536]{1,0:T(8,128)(2,1)} %dynamic-slice_bitcast_fusion.3), channel_id=1, source_target_pairs={{0,2},{2,0},{1,3},{3,1},{4,6},{6,4},{5,7},{7,5},{8,10},{10,8},{9,1... | collective-permute-start | bytes 2359304 | tf_op jit(solution)/shard_map/ppermute | solution.py:499
  362.1 18.2 %collective-permute-start.39 = (bf16[48,1536]{1,0:T(8,128)(2,1)S(1)}, bf16[48,1536]{1,0:T(8,128)(2,1)S(1)}, u32[]{:S(2)}, u32[]{:S(2)}) collective-permute-start(bf16[48,1536]{1,0:T(8,128)(2,1)S(1)} %dynamic-slice_bitcast_fusion.11), channel_id=1, source_target_pairs={{0,4},{4,0},{1,5},{5,1},{2,6},{6,2},{3,7},{7,3},{8,12},{12,8},{9,1... | collective-permute-start | bytes 442376 | tf_op jit(solution)/shard_map/ppermute | solution.py:499
  (65 other events, 592.7 us)
Sparse Core Ops, SparseCore 0:
  17.2 76.4 all-gather.1
  189.3 87.9 reduce-scatter.3
